TPU v7x, 32 devices: a whole 2x2x4 slice. The times are simulated.
32 devices in a mesh: expert: 8 (over y, x, core), head: 4 (over z).
Axes of the slice: x: 2, y: 2, z: 4, core: 2. Of those that a mesh axis runs over, the one named last changes fastest.
Arguments:
- short_x: bfloat16 [256, 64, 512], P('expert'), may hold values from -45 to 45
- long_x: bfloat16 [64, 256, 512], P('expert'), may hold values from -45 to 45
- short_cot: bfloat16 [256, 64, 512], P('expert'), may hold values from -10 to 10
- long_cot: bfloat16 [64, 256, 512], P('expert'), may hold values from -10 to 10
- short_len: int32 [256], P('expert'), may hold values from 9 to 64, as said below
- long_len: int32 [64], P('expert'), may hold values from 33 to 256, as said below
- short_task: int32 [256], P('expert'), may hold values from 0 to 7, as said below
- long_task: int32 [64], P('expert'), may hold values from 0 to 7, as said below
- expert_ids: int32 [8, 2], replicated, may hold values from 0 to 7, as said below
- ln_gain: float32 [2, 512], replicated, may hold values from 0.5 to 1.5
- ln_bias: float32 [2, 512], replicated, may hold values from -1.75 to 1.75
- w_qkv: bfloat16 [3, 512, 512], P(None, None, 'head'), may hold values from -0.25 to 0.25
- b_qv: float32 [2, 512], P(None, 'head'), may hold values from -1.75 to 1.75
- w_attn_out: bfloat16 [512, 512], P('head'), may hold values from -1 to 1
- b_attn_out: float32 [512], replicated, may hold values from -1.75 to 1.75
- w_up: bfloat16 [8, 512, 2048], P('expert'), may hold values from -0.25 to 0.25
- b_up: float32 [8, 2048], P('expert'), may hold values from -0.625 to 0.625
- w_down: bfloat16 [8, 2048, 512], P('expert'), may hold values from -0.125 to 0.125
- b_down: float32 [8, 512], P('expert'), may hold values from -0.625 to 0.625
- task_emb: float32 [8, 512], replicated, may hold values from -6 to 6
- gate_w: float32 [512, 8], replicated, may hold values from -0.1875 to 0.1875
Outputs:
- short_out: bfloat16 [256, 64, 512], P(('expert', 'head'))
- long_out: bfloat16 [64, 256, 512], P(('expert', 'head'))
- short_dx: float32 [256, 64, 512], P(('expert', 'head'))
- long_dx: float32 [64, 256, 512], P(('expert', 'head'))
- grad_ln_gain: float32 [2, 512], replicated
- grad_ln_bias: float32 [2, 512], replicated
- grad_w_qkv: float32 [3, 512, 512], P(None, None, 'head')
- grad_b_qv: float32 [2, 512], P(None, 'head')
- grad_w_attn_out: float32 [512, 512], P('head')
- grad_b_attn_out: float32 [512], replicated
- grad_w_up: float32 [8, 512, 2048], P('expert', None, 'head')
- grad_b_up: float32 [8, 2048], P('expert', 'head')
- grad_w_down: float32 [8, 2048, 512], P('expert', 'head')
- grad_b_down: float32 [8, 512], P('expert', 'head')
- grad_task_emb: float32 [8, 512], replicated
- grad_gate_w: float32 [512, 8], replicated
Inputs may be any that keep to these rules, and one draw needn't show every extreme that they name: `short_len`: in every block of 32 consecutive short sentences one has length 64. `long_len`: in every block of 8 consecutive long sentences one has length 256. `short_task`: in every block of 32 consecutive short sentences every task occurs exactly 32 / 8 times. `long_task`: in every block of 8 consecutive long sentences the tasks are all even or all odd, and each task of that parity occurs exactly 2 * 8 / 8 times. The first column is a permutation of the experts and expert_ids[t, 1] = expert_ids[(t + 1) % 8, 0]; so in every block of sentences above each expert is named by exactly 8 short and 2 long sentences.
All inputs are finite; a program needn't handle non-finite values.
Results may differ from a plain program's by a relative error of at most 0.018.
Values may be sent and summed in bfloat16 or wider, within the bound.
No kernel may reach another device: no remote copies, remote signals or barrier semaphores. Data moves between devices by JAX's collectives and lax.ppermute only.
A program may use at most 256 MiB of HBM per device.

v0:
```python
import jax
import jax.numpy as jnp
from jax import lax
from jax.sharding import PartitionSpec as P

HEAD_DIM = 64


HIGHEST = lax.Precision.HIGHEST
CONTRACT_ROWS = (((0,), (0,)), ((), ()))
CONTRACT_COLS = (((1,), (1,)), ((), ()))


def layer_norm(values, gain, shift):
    centred = values - jnp.mean(values, axis=-1, keepdims=True)
    spread = jnp.mean(centred * centred, axis=-1, keepdims=True)
    return centred * lax.rsqrt(spread + 1e-05) * gain + shift


def lookup(table, index):
    hits = index[..., None] == jnp.arange(table.shape[0], dtype=jnp.int32)
    return jnp.sum(jnp.where(hits, table, jnp.zeros((), table.dtype)), axis=-1)


def route_slots(tasks, expert_ids, capacity, experts):
    task_hits = tasks[:, None] == jnp.arange(expert_ids.shape[0], dtype=jnp.int32)
    chosen = jnp.sum(jnp.where(task_hits[:, :, None], expert_ids[None, :, :], 0), axis=1).reshape(
        -1
    )
    routes = chosen.shape[0]
    owner_hits = (chosen[:, None] == jnp.arange(experts, dtype=jnp.int32)).astype(jnp.int32)
    earlier = jnp.cumsum(owner_hits, axis=0) - owner_hits
    ranking = jnp.sum(earlier * owner_hits, axis=1)
    slot_key = chosen * capacity + ranking
    slot_hits = slot_key[:, None] == jnp.arange(experts * capacity, dtype=jnp.int32)
    return jnp.sum(jnp.where(slot_hits, jnp.arange(routes, dtype=jnp.int32)[:, None], 0), axis=0)


def masked_scores(queries, key_rows, lengths):
    positions = key_rows.shape[1]
    scores = jnp.einsum(
        "blhd,bmhd->bhlm", queries, key_rows, preferred_element_type=jnp.float32
    ) * HEAD_DIM ** (-0.5)
    visible = (
        jnp.arange(positions, dtype=jnp.int32)[None, None, None, :] < lengths[:, None, None, None]
    )
    return jnp.where(visible, scores, -1e30)


def attend(normed, lengths, weights, biases, head_count):
    sentences, positions, features = normed.shape
    flattened = normed.reshape(-1, features)
    shape_heads = (sentences, positions, head_count, HEAD_DIM)

    def project(index, offset):
        return (
            (jnp.dot(flattened, weights[index], preferred_element_type=jnp.float32) + offset)
            .astype(jnp.bfloat16)
            .reshape(shape_heads)
        )

    queries = project(0, biases[0])
    key_rows = project(1, 0.0)
    values = project(2, biases[1])
    scores = masked_scores(queries, key_rows, lengths)
    highest = jnp.max(scores, axis=-1, keepdims=True)
    shifted = jnp.exp(scores - highest)
    totals = jnp.sum(shifted, axis=-1, keepdims=True)
    attn_probs = (shifted / totals).astype(jnp.bfloat16)
    log_total = highest + jnp.log(totals)
    context = jnp.einsum(
        "bhlm,bmhd->blhd", attn_probs, values, preferred_element_type=jnp.float32
    ).astype(jnp.bfloat16)
    return (queries, key_rows, values, context.reshape(sentences, positions, -1), log_total)


def attend_back(normed, lengths, kept, grad_out, weights, out_weight):
    queries, key_rows, values, context, log_total = kept
    features = normed.shape[-1]
    head_cols = context.shape[-1]
    grad_flat = grad_out.reshape(-1, features)
    context_flat = context.reshape(-1, head_cols)
    grad_context = (
        lax.dot_general(grad_flat, out_weight, CONTRACT_COLS, preferred_element_type=jnp.float32)
        .astype(jnp.bfloat16)
        .reshape(queries.shape)
    )
    grad_out_weight = lax.dot_general(
        context_flat, grad_flat, CONTRACT_ROWS, preferred_element_type=jnp.float32
    )
    probs = jnp.exp(masked_scores(queries, key_rows, lengths) - log_total)
    grad_probs = jnp.einsum(
        "blhd,bmhd->bhlm", grad_context, values, preferred_element_type=jnp.float32
    )
    grad_values = jnp.einsum(
        "bhlm,blhd->bmhd",
        probs.astype(jnp.bfloat16),
        grad_context,
        preferred_element_type=jnp.float32,
    ).astype(jnp.bfloat16)
    grad_scores = (
        probs * (grad_probs - jnp.sum(probs * grad_probs, axis=-1, keepdims=True))
    ).astype(jnp.bfloat16)
    scaling = HEAD_DIM ** (-0.5)
    grad_queries = (
        jnp.einsum("bhlm,bmhd->blhd", grad_scores, key_rows, preferred_element_type=jnp.float32)
        * scaling
    ).astype(jnp.bfloat16)
    grad_keys = (
        jnp.einsum("bhlm,blhd->bmhd", grad_scores, queries, preferred_element_type=jnp.float32)
        * scaling
    ).astype(jnp.bfloat16)
    normed_flat = normed.reshape(-1, features)
    members = [member.reshape(-1, head_cols) for member in (grad_queries, grad_keys, grad_values)]
    grad_weights = jnp.stack(
        [
            lax.dot_general(normed_flat, member, CONTRACT_ROWS, preferred_element_type=jnp.float32)
            for member in members
        ]
    )
    grad_biases = jnp.stack(
        [
            jnp.sum(members[0].astype(jnp.float32), axis=0),
            jnp.sum(members[2].astype(jnp.float32), axis=0),
        ]
    )
    grad_normed = lax.dot_general(
        members[0], weights[0], CONTRACT_COLS, preferred_element_type=jnp.float32
    )
    grad_normed = grad_normed + lax.dot_general(
        members[1], weights[1], CONTRACT_COLS, preferred_element_type=jnp.float32
    )
    grad_normed = grad_normed + lax.dot_general(
        members[2], weights[2], CONTRACT_COLS, preferred_element_type=jnp.float32
    )
    return (grad_normed.reshape(normed.shape), grad_weights, grad_out_weight, grad_biases)


def group_rows(first_rows, second_rows):
    return (
        lax.all_gather(first_rows, "head", axis=0, tiled=True),
        lax.all_gather(second_rows, "head", axis=0, tiled=True),
    )


def per_device(
    short_x,
    long_x,
    short_cot,
    long_cot,
    short_len,
    long_len,
    short_task,
    long_task,
    expert_ids,
    ln_gain,
    ln_bias,
    w_qkv,
    b_qv,
    w_attn_out,
    b_attn_out,
    w_up,
    b_up,
    w_down,
    b_down,
    task_emb,
    gate_w,
):
    heads_here = lax.axis_size("head")
    head_place = lax.axis_index("head")
    experts = lax.axis_size("expert")
    short_group, short_span, features = short_x.shape
    long_group, long_span = (long_x.shape[0], long_x.shape[1])
    short_dev = short_group // heads_here
    long_dev = long_group // heads_here
    hidden_width = w_up.shape[2]
    tasks_total = expert_ids.shape[0]
    cap_short = 2 * short_group // experts
    cap_long = 2 * long_group // experts
    piece_rows = (cap_short * short_span + cap_long * long_span) // heads_here
    short_total = short_group * short_span
    all_rows = short_total + long_group * long_span
    expert_hits = (expert_ids[:, :, None] == jnp.arange(experts, dtype=jnp.int32)).astype(
        jnp.float32
    )
    chosen_cols = jnp.einsum("tke,de->tkd", expert_hits, gate_w, precision=HIGHEST)
    gate_probs = jax.nn.softmax(jnp.sum(task_emb[:, None, :] * chosen_cols, axis=-1), axis=-1)
    short_slots = route_slots(short_task, expert_ids, cap_short, experts)
    long_slots = route_slots(long_task, expert_ids, cap_long, experts)
    offsets = head_place * piece_rows + jnp.arange(piece_rows, dtype=jnp.int32)
    owners = jnp.arange(experts, dtype=jnp.int32)[:, None]
    in_short = jnp.broadcast_to(offsets < cap_short * short_span, (experts, piece_rows))
    short_pos = offsets % short_span
    long_offset = jnp.maximum(offsets - cap_short * short_span, 0)
    long_pos = long_offset % long_span
    short_route = lookup(
        short_slots, owners * cap_short + jnp.minimum(offsets // short_span, cap_short - 1)
    )
    long_route = lookup(
        long_slots, owners * cap_long + jnp.minimum(long_offset // long_span, cap_long - 1)
    )
    short_sent = short_route // 2
    long_sent = long_route // 2
    position = jnp.where(in_short, short_pos, long_pos)
    target = jnp.where(
        in_short,
        short_sent * short_span + short_pos,
        short_total + long_sent * long_span + long_pos,
    )
    task_rows = jnp.where(in_short, lookup(short_task, short_sent), lookup(long_task, long_sent))
    length_rows = jnp.where(in_short, lookup(short_len, short_sent), lookup(long_len, long_sent))
    live_rows = (position < length_rows).astype(jnp.float32)
    gate_index = task_rows * 2 + jnp.where(in_short, short_route % 2, long_route % 2)
    gate_rows = lookup(gate_probs.reshape(-1), gate_index)
    short_mask = (jnp.arange(short_span, dtype=jnp.int32)[None, :] < short_len[:, None]).astype(
        jnp.float32
    )[:, :, None]
    long_mask = (jnp.arange(long_span, dtype=jnp.int32)[None, :] < long_len[:, None]).astype(
        jnp.float32
    )[:, :, None]
    short_start = head_place * short_dev
    long_start = head_place * long_dev
    own_short_mask = lax.dynamic_slice_in_dim(short_mask, short_start, short_dev, 0)
    own_long_mask = lax.dynamic_slice_in_dim(long_mask, long_start, long_dev, 0)
    short_in = short_x.astype(jnp.float32)
    long_in = long_x.astype(jnp.float32)
    own_short_in = lax.dynamic_slice_in_dim(short_in, short_start, short_dev, 0)
    own_long_in = lax.dynamic_slice_in_dim(long_in, long_start, long_dev, 0)
    attn_qkv, attn_qv, attn_out_w = (w_qkv, b_qv, w_attn_out)
    short_src, long_src = (short_in, long_in)
    short_lens, long_lens = (short_len, long_len)
    head_cols = attn_qkv.shape[2]
    head_count = head_cols // HEAD_DIM
    short_normed = layer_norm(short_src, ln_gain[0], ln_bias[0]).astype(jnp.bfloat16)
    long_normed = layer_norm(long_src, ln_gain[0], ln_bias[0]).astype(jnp.bfloat16)
    short_kept = attend(short_normed, short_lens, attn_qkv, attn_qv, head_count)
    long_kept = attend(long_normed, long_lens, attn_qkv, attn_qv, head_count)
    short_part = jnp.dot(
        short_kept[3].reshape(-1, head_cols), attn_out_w, preferred_element_type=jnp.float32
    ).reshape(short_src.shape)
    long_part = jnp.dot(
        long_kept[3].reshape(-1, head_cols), attn_out_w, preferred_element_type=jnp.float32
    ).reshape(long_src.shape)
    short_sum, long_sum = (
        lax.psum(short_part.astype(jnp.bfloat16), "head").astype(jnp.float32),
        lax.psum(long_part.astype(jnp.bfloat16), "head").astype(jnp.float32),
    )
    short_mid = short_in + short_mask * (short_sum + b_attn_out)
    long_mid = long_in + long_mask * (long_sum + b_attn_out)
    short_mixin = layer_norm(short_mid, ln_gain[1], ln_bias[1]).astype(jnp.bfloat16)
    long_mixin = layer_norm(long_mid, ln_gain[1], ln_bias[1]).astype(jnp.bfloat16)
    own_short_mid = lax.dynamic_slice_in_dim(short_mid, short_start, short_dev, 0)
    own_long_mid = lax.dynamic_slice_in_dim(long_mid, long_start, long_dev, 0)
    mixin_rows = jnp.concatenate(
        [short_mixin.reshape(-1, features), long_mixin.reshape(-1, features)], axis=0
    )
    outgoing = mixin_rows[target]
    received = lax.all_to_all(outgoing, "expert", split_axis=0, concat_axis=0, tiled=True)
    inputs = received.reshape(-1, features)
    gelu_in = jnp.dot(inputs, w_up[0], preferred_element_type=jnp.float32) + b_up[0]
    hidden = jax.nn.gelu(gelu_in).astype(jnp.bfloat16)
    output = (jnp.dot(hidden, w_down[0], preferred_element_type=jnp.float32) + b_down[0]).astype(
        jnp.bfloat16
    )
    returned = lax.all_to_all(
        output.reshape(received.shape), "expert", split_axis=0, concat_axis=0, tiled=True
    )
    wide_shape = received.shape[:2] + (hidden_width,)
    packed = (returned, received, hidden.reshape(wide_shape), gelu_in.reshape(wide_shape))
    returned = packed[0]
    received = packed[1]
    contrib = (gate_rows[:, :, None] * returned.astype(jnp.float32)).reshape(-1, features)
    mixed_rows = jnp.zeros((all_rows, features), jnp.float32).at[target.reshape(-1)].add(contrib)
    short_moe, long_moe = (
        lax.psum_scatter(
            mixed_rows[:short_total].reshape(short_in.shape).astype(jnp.bfloat16),
            "head",
            scatter_dimension=0,
            tiled=True,
        ).astype(jnp.float32),
        lax.psum_scatter(
            mixed_rows[short_total:].reshape(long_in.shape).astype(jnp.bfloat16),
            "head",
            scatter_dimension=0,
            tiled=True,
        ).astype(jnp.float32),
    )
    short_out = (own_short_mid + own_short_mask * short_moe).astype(jnp.bfloat16)
    long_out = (own_long_mid + own_long_mask * long_moe).astype(jnp.bfloat16)
    cot_rows = jnp.concatenate(
        [short_cot.reshape(-1, features), long_cot.reshape(-1, features)], axis=0
    )
    cot_picked = cot_rows[target].astype(jnp.float32)
    grad_sent = ((gate_rows * live_rows)[:, :, None] * cot_picked).astype(jnp.bfloat16)
    gate_terms = live_rows * jnp.sum(cot_picked * returned.astype(jnp.float32), axis=-1)
    gate_part = jnp.sum(
        jnp.where(
            gate_index[:, :, None] == jnp.arange(2 * tasks_total, dtype=jnp.int32),
            gate_terms[:, :, None],
            0.0,
        ),
        axis=(0, 1),
    )
    grad_arrived = lax.all_to_all(grad_sent, "expert", split_axis=0, concat_axis=0, tiled=True)
    inputs = received.reshape(-1, features)
    hidden = packed[2].reshape(-1, hidden_width)
    gelu_in = packed[3].reshape(-1, hidden_width)
    grad_output = grad_arrived.reshape(-1, features)
    grad_hidden = lax.dot_general(
        grad_output, w_down[0], CONTRACT_COLS, preferred_element_type=jnp.float32
    )
    grad_gelu = jax.vjp(jax.nn.gelu, gelu_in)[1](grad_hidden)[0].astype(jnp.bfloat16)
    grad_up_w = lax.dot_general(
        inputs, grad_gelu, CONTRACT_ROWS, preferred_element_type=jnp.float32
    )
    grad_up_b = jnp.sum(grad_gelu.astype(jnp.float32), axis=0)
    grad_down_w = lax.dot_general(
        hidden, grad_output, CONTRACT_ROWS, preferred_element_type=jnp.float32
    )
    grad_down_b = jnp.sum(grad_output.astype(jnp.float32), axis=0)
    grad_inputs = (
        lax.dot_general(grad_gelu, w_up[0], CONTRACT_COLS, preferred_element_type=jnp.float32)
        .astype(jnp.bfloat16)
        .reshape(received.shape)
    )
    grad_home = lax.all_to_all(grad_inputs, "expert", split_axis=0, concat_axis=0, tiled=True)
    shard_up_w, shard_up_b, shard_down_w, shard_down_b = (
        lax.psum_scatter(
            grad_up_w[None].astype(jnp.bfloat16), "head", scatter_dimension=2, tiled=True
        ).astype(jnp.float32),
        lax.psum_scatter(
            grad_up_b[None].astype(jnp.bfloat16), "head", scatter_dimension=1, tiled=True
        ).astype(jnp.float32),
        lax.psum_scatter(
            grad_down_w[None].astype(jnp.bfloat16), "head", scatter_dimension=1, tiled=True
        ).astype(jnp.float32),
        lax.psum_scatter(
            grad_down_b[None].astype(jnp.bfloat16), "head", scatter_dimension=1, tiled=True
        ).astype(jnp.float32),
    )
    grad_mixin = (
        jnp.zeros((all_rows, features), jnp.float32)
        .at[target.reshape(-1)]
        .add(grad_home.reshape(-1, features).astype(jnp.float32))
    )
    short_dmix, long_dmix = (
        lax.psum_scatter(
            grad_mixin[:short_total].reshape(short_in.shape).astype(jnp.bfloat16),
            "head",
            scatter_dimension=0,
            tiled=True,
        ).astype(jnp.float32),
        lax.psum_scatter(
            grad_mixin[short_total:].reshape(long_in.shape).astype(jnp.bfloat16),
            "head",
            scatter_dimension=0,
            tiled=True,
        ).astype(jnp.float32),
    )
    short_dmid, short_gain_two, short_shift_two = jax.vjp(
        layer_norm, own_short_mid, ln_gain[1], ln_bias[1]
    )[1](short_dmix)
    long_dmid, long_gain_two, long_shift_two = jax.vjp(
        layer_norm, own_long_mid, ln_gain[1], ln_bias[1]
    )[1](long_dmix)
    short_dmid = short_dmid + lax.dynamic_slice_in_dim(short_cot, short_start, short_dev, 0).astype(
        jnp.float32
    )
    long_dmid = long_dmid + lax.dynamic_slice_in_dim(long_cot, long_start, long_dev, 0).astype(
        jnp.float32
    )
    short_dattn = (own_short_mask * short_dmid).astype(jnp.bfloat16)
    long_dattn = (own_long_mask * long_dmid).astype(jnp.bfloat16)
    bias_out_grad = jnp.sum(short_dattn.astype(jnp.float32), axis=(0, 1)) + jnp.sum(
        long_dattn.astype(jnp.float32), axis=(0, 1)
    )
    attn_short_grad, attn_long_grad = group_rows(short_dattn, long_dattn)
    short_back = attend_back(
        short_normed, short_lens, short_kept, attn_short_grad, attn_qkv, attn_out_w
    )
    long_back = attend_back(long_normed, long_lens, long_kept, attn_long_grad, attn_qkv, attn_out_w)
    short_dnormed, long_dnormed = (
        lax.psum_scatter(
            short_back[0].astype(jnp.bfloat16), "head", scatter_dimension=0, tiled=True
        ).astype(jnp.float32),
        lax.psum_scatter(
            long_back[0].astype(jnp.bfloat16), "head", scatter_dimension=0, tiled=True
        ).astype(jnp.float32),
    )
    short_dln, short_gain_one, short_shift_one = jax.vjp(
        layer_norm, own_short_in, ln_gain[0], ln_bias[0]
    )[1](short_dnormed)
    long_dln, long_gain_one, long_shift_one = jax.vjp(
        layer_norm, own_long_in, ln_gain[0], ln_bias[0]
    )[1](long_dnormed)
    short_dx = short_dmid + short_dln
    long_dx = long_dmid + long_dln
    qkv_terms = short_back[1] + long_back[1]
    out_terms = short_back[2] + long_back[2]
    bias_terms = short_back[3] + long_back[3]
    grad_qkv, grad_attn_weight, grad_qv = (
        lax.psum(qkv_terms.astype(jnp.bfloat16), "expert").astype(jnp.float32),
        lax.psum(out_terms.astype(jnp.bfloat16), "expert").astype(jnp.float32),
        lax.psum(bias_terms.astype(jnp.bfloat16), "expert").astype(jnp.float32),
    )
    gain_grads = jnp.stack([short_gain_one + long_gain_one, short_gain_two + long_gain_two])
    shift_grads = jnp.stack([short_shift_one + long_shift_one, short_shift_two + long_shift_two])
    grad_gain, grad_shift, grad_bias_out, gate_total = lax.psum(
        (gain_grads, shift_grads, bias_out_grad, gate_part), ("expert", "head")
    )
    gate_grad = gate_total.reshape(tasks_total, 2)
    logit_grad = gate_probs * (gate_grad - jnp.sum(gate_probs * gate_grad, axis=-1, keepdims=True))
    grad_task = jnp.sum(logit_grad[:, :, None] * chosen_cols, axis=1)
    grad_gate = jnp.einsum("tke,tk,td->de", expert_hits, logit_grad, task_emb, precision=HIGHEST)
    return (
        short_out,
        long_out,
        short_dx,
        long_dx,
        grad_gain,
        grad_shift,
        grad_qkv,
        grad_qv,
        grad_attn_weight,
        grad_bias_out,
        shard_up_w,
        shard_up_b,
        shard_down_w,
        shard_down_b,
        grad_task,
        grad_gate,
    )


def solution(mesh):
    return jax.shard_map(
        per_device,
        mesh=mesh,
        in_specs=(
            P("expert", None, None),
            P("expert", None, None),
            P("expert", None, None),
            P("expert", None, None),
            P("expert"),
            P("expert"),
            P("expert"),
            P("expert"),
            P(),
            P(),
            P(),
            P(None, None, "head"),
            P(None, "head"),
            P("head", None),
            P(),
            P("expert", None, None),
            P("expert", None),
            P("expert", None, None),
            P("expert", None),
            P(),
            P(),
        ),
        out_specs=(
            P(("expert", "head"), None, None),
            P(("expert", "head"), None, None),
            P(("expert", "head"), None, None),
            P(("expert", "head"), None, None),
            P(),
            P(),
            P(None, None, "head"),
            P(None, "head"),
            P("head", None),
            P(),
            P("expert", None, "head"),
            P("expert", "head"),
            P("expert", "head", None),
            P("expert", "head"),
            P(),
            P(),
        ),
        check_vma=False,
    )
```

profile of v0, /device:TPU:0, one launch (start us, length us, event | category | flops | bytes accessed | tf_op | source)
XLA Modules:
  0.0 1048.8 jit_solution(1180196379777907603)
XLA Ops:
  10.9 2.4 multiply_reduce_fusion.2
  25.7 2.4 reshape.1343
  29.9 3.2 reshape.1344
  33.1 2.3 copy.160
  35.5 3.4 reshape.1345
  38.8 2.3 copy.161
  41.2 3.3 reshape.1271
  44.5 3.6 copy.170
  48.1 3.4 reshape.1272
  51.6 3.2 reshape.1270
  67.9 156.1 %all-reduce.8.cloned.1.call-done = (bf16[8,256,512]{2,1,0:T(8,128)(2,1)}, bf16[32,64,512]{2,1,0:T(8,128)(2,1)}) async-done(((bf16[8,256,512]{2,1,0:T(8,128)(2,1)}, bf16[32,64,512]{2,1,0:T(8,128)(2,1)}), (bf16[8,256,512]{2,1,0:T(8,128)(2,1)}, bf16[32,64,512]{2,1,0:T(8,128)(2,1)})) %all-reduce.8.cloned.1.call-update) | async-done | bytes 4194320 | tf_op jit(solution)/shard_map/psum | solution.py:246
  224.1 3.3 fusion.150
  228.2 2.3 copy-done.11
  235.5 2.2 pad_maximum_fusion
  237.7 12.0 %gather_fusion = bf16[2048,512]{1,0:T(8,128)(2,1)} fusion(bf16[4096,512]{1,0:T(8,128)(2,1)} %pad_maximum_fusion, s32[2048]{0:T(1024)S(1)} %broadcast_clamp_fusion), kind=kCustom, calls=%fused_computation | custom fusion | bytes 4202496 | tf_op jit(solution)/shard_map/gather | solution.py:257
  249.7 30.4 %all_to_all.20 = bf16[8,256,512]{2,1,0:T(8,128)(2,1)S(1)} all-to-all(bf16[8,256,512]{2,1,0:T(8,128)(2,1)} %bitcast.309), channel_id=1, replica_groups=mesh['expert'=8,'head'=4] {'expert'}, dimensions={0} | all-to-all | bytes 4194304 | tf_op jit(solution)/shard_map/all_to_all | solution.py:258
  280.1 10.8 %multiply_convert_fusion = (bf16[2048,2048]{1,0:T(8,128)(2,1)S(1)}, f32[2048,2048]{1,0:T(8,128)}) fusion(f32[2048]{0:T(1024)S(1)} %bitcast.397, bf16[2048,512]{1,0:T(8,128)(2,1)S(1)} %bitcast.336, bf16[1,512,2048]{2,1,0:T(8,128)(2,1)S(1)} %copy-done), kind=kOutput, calls=%fused_computation.13 | convolution fusion | flops 4336910336 | bytes 29368320 | tf_op jit(solution)/shard_map/dot_general | solution.py:260
  290.9 5.7 add_convert_fusion.2
  296.6 4.3 all-to-all-start.1
  300.9 4.4 pad_maximum_fusion.1
  305.4 12.0 %gather_fusion.1 = bf16[2048,512]{1,0:T(8,128)(2,1)} fusion(bf16[4096,512]{1,0:T(8,128)(2,1)} %pad_maximum_fusion.1, s32[2048]{0:T(1024)S(1)} %broadcast_clamp_fusion), kind=kCustom, calls=%fused_computation.1 | custom fusion | bytes 4202496 | tf_op jit(solution)/shard_map/gather | solution.py:293
  318.9 8.7 all-to-all-done.1
  327.6 3.0 fusion.8
  331.7 29.4 %all_to_all.21 = bf16[8,256,512]{2,1,0:T(8,128)(2,1)S(1)} all-to-all(bf16[8,256,512]{2,1,0:T(8,128)(2,1)S(1)} %fusion.7), channel_id=1, replica_groups=mesh['expert'=8,'head'=4] {'expert'}, dimensions={0} | all-to-all | bytes 4194304 | tf_op jit(solution)/shard_map/all_to_all | solution.py:304
  361.1 18.6 %fusion.157 = (bf16[2048]{0:T(1024)(128)(2,1)S(1)}, bf16[2048,2048]{1,0:T(8,128)(2,1)S(1)}) fusion(f32[2048,2048]{1,0:T(8,128)} %get-tuple-element.89, f32[2048]{0:T(1024)S(1)} %bitcast.398, bf16[2048,512]{1,0:T(8,128)(2,1)S(1)} %bitcast.310, bf16[1,2048,512]{2,1,0:T(8,128)(2,1)S(1)} %copy-done.91), kind=kOutput, calls=%fused_computation.385 | convolution fusion | flops 4387239936 | bytes 29372416 | tf_op jit(solution)/shard_map/dot_general | solution.py:309
  379.7 6.2 convolution_convert_fusion.2
  385.9 3.6 all-to-all-start.3
  389.8 26.3 %all-to-all-done.3 = bf16[8,256,512]{2,1,0:T(8,128)(2,1)S(1)} async-done(((bf16[8,256,512]{2,1,0:T(8,128)(2,1)}), bf16[8,256,512]{2,1,0:T(8,128)(2,1)S(1)}, u32[]{:S(2)}, u32[]{:S(2)}) %all-to-all-start.3) | async-done | bytes 2097184 | tf_op jit(solution)/shard_map/all_to_all | solution.py:326
  416.1 16.5 %scatter_custom_fusion.1 = f32[4096,512]{1,0:T(8,128)} fusion(s32[2048]{0:T(1024)S(1)} %bitcast.394, bf16[2048,512]{1,0:T(8,128)(2,1)S(1)} %bitcast.322, f32[]{:T(128)} %constant.165.clone.1), kind=kCustom, calls=%fused_computation.21 | custom fusion | flops 2097152 | bytes 10485764 | tf_op jit(solution)/shard_map/scatter-add | solution.py:344
  432.6 3.9 convert.12
  436.6 2.2 fusion.151
  438.9 3.9 convert_multiply_fusion.2
  442.7 17.1 %scatter_custom_fusion = f32[4096,512]{1,0:T(8,128)} fusion(s32[2048]{0:T(1024)S(1)} %bitcast.395, f32[2048,512]{1,0:T(8,128)} %bitcast.335, f32[]{:T(128)} %constant.165.clone.1), kind=kCustom, calls=%fused_computation.40 | custom fusion | flops 1048576 | bytes 8389120 | tf_op jit(solution)/shard_map/scatter-add | solution.py:273
  459.9 3.9 convert.11
  463.8 2.3 fusion.152
  468.7 11.3 %reduce-scatter.19.cloned.1.call-done = bf16[8,64,512]{2,1,0:T(8,128)(2,1)} async-done(((bf16[32,64,512]{2,1,0:T(8,128)(2,1)}), bf16[8,64,512]{2,1,0:T(8,128)(2,1)}) %reduce-scatter.19.cloned.1.call-update) | async-done | bytes 524304 | tf_op jit(solution)/shard_map/reduce_scatter | solution.py:347
  484.0 41.6 %reduce-scatter.15.cloned.1.call-done = bf16[8,64,512]{2,1,0:T(8,128)(2,1)} async-done(((bf16[32,64,512]{2,1,0:T(8,128)(2,1)}), bf16[8,64,512]{2,1,0:T(8,128)(2,1)}) %reduce-scatter.15.cloned.1.call-update) | async-done | bytes 524304 | tf_op jit(solution)/shard_map/reduce_scatter | solution.py:275
  525.6 3.3 convert_reduce_fusion.9
  530.4 40.6 %reduce-scatter.23.cloned.1.call-done = bf16[2,256,512]{2,1,0:T(8,128)(2,1)} async-done(((bf16[8,256,512]{2,1,0:T(8,128)(2,1)}), bf16[2,256,512]{2,1,0:T(8,128)(2,1)}) %reduce-scatter.23.cloned.1.call-update) | async-done | bytes 524304 | tf_op jit(solution)/shard_map/reduce_scatter | solution.py:353
  574.9 41.5 %reduce-scatter.17.cloned.1.call-done = bf16[2,256,512]{2,1,0:T(8,128)(2,1)} async-done(((bf16[8,256,512]{2,1,0:T(8,128)(2,1)}), bf16[2,256,512]{2,1,0:T(8,128)(2,1)}) %reduce-scatter.17.cloned.1.call-update) | async-done | bytes 524304 | tf_op jit(solution)/shard_map/reduce_scatter | solution.py:281
  616.4 3.2 convert_reduce_fusion.8
  622.6 10.4 fusion.16
  634.8 2.7 reshape_reshape.8
  639.8 9.5 fusion.17
  649.6 13.5 %all-gather.3.cloned.1.call-done = bf16[32,64,512]{2,1,0:T(8,128)(2,1)} async-done(((bf16[8,64,512]{2,1,0:T(8,128)(2,1)}), bf16[32,64,512]{2,1,0:T(8,128)(2,1)}) %all-gather.3.cloned.1.call-update) | async-done | bytes 2097168 | tf_op jit(solution)/shard_map/all_gather | solution.py:141
  663.1 3.1 convolution_convert_fusion.4
  666.2 2.4 reshape.1289
  676.8 2.8 copy.169
  686.9 22.6 %all-gather.5.cloned.1.call-done = bf16[8,256,512]{2,1,0:T(8,128)(2,1)} async-done(((bf16[2,256,512]{2,1,0:T(8,128)(2,1)}), bf16[8,256,512]{2,1,0:T(8,128)(2,1)}) %all-gather.5.cloned.1.call-update) | async-done | bytes 2097168 | tf_op jit(solution)/shard_map/all_gather | solution.py:142
  709.5 2.3 convolution_convert_fusion.3
  713.1 3.4 multiply_reduce_fusion
  728.5 2.7 fusion.87
  731.2 2.7 fusion.81
  734.0 5.7 add_convert_fusion.1
  753.5 42.7 %reduce-scatter.27.cloned.1.call-done = bf16[1,512,512]{2,1,0:T(8,128)(2,1)} async-done(((bf16[1,512,2048]{2,1,0:T(8,128)(2,1)}), bf16[1,512,512]{2,1,0:T(8,128)(2,1)}) %reduce-scatter.27.cloned.1.call-update) | async-done | bytes 524304 | tf_op jit(solution)/shard_map/reduce_scatter | solution.py:328
  798.3 43.5 %reduce-scatter.29.cloned.1.call-done = bf16[1,512,512]{2,1,0:T(8,128)(2,1)} async-done(((bf16[1,2048,512]{2,1,0:T(8,128)(2,1)}), bf16[1,512,512]{2,1,0:T(8,128)(2,1)}) %reduce-scatter.29.cloned.1.call-update) | async-done | bytes 524304 | tf_op jit(solution)/shard_map/reduce_scatter | solution.py:334
  841.8 2.1 convert_element_type.417
  844.4 13.5 %psum.68 = bf16[2,128]{1,0:T(2,128)(2,1)S(1)} all-reduce(bf16[2,128]{1,0:T(2,128)(2,1)S(1)} %fusion.137), channel_id=1, replica_groups=mesh['expert'=8,'head'=4] {'expert'}, use_global_device_ids=true, to_apply=%region_73.74 | all-reduce | flops 256 | bytes 1024 | tf_op jit(solution)/shard_map/psum | solution.py:404
  858.5 41.0 %all-reduce.6.cloned.1.call-done = (bf16[3,512,128]{2,1,0:T(8,128)(2,1)}, bf16[128,512]{1,0:T(8,128)(2,1)}) async-done(((bf16[3,512,128]{2,1,0:T(8,128)(2,1)}, bf16[128,512]{1,0:T(8,128)(2,1)}), (bf16[3,512,128]{2,1,0:T(8,128)(2,1)}, bf16[128,512]{1,0:T(8,128)(2,1)})) %all-reduce.6.cloned.1.call-update) | async-done | bytes 524304 | tf_op jit(solution)/shard_map/psum | solution.py:402
  903.0 42.0 %reduce-scatter.21.cloned.1.call-done = bf16[8,64,512]{2,1,0:T(8,128)(2,1)} async-done(((bf16[32,64,512]{2,1,0:T(8,128)(2,1)}), bf16[8,64,512]{2,1,0:T(8,128)(2,1)}) %reduce-scatter.21.cloned.1.call-update) | async-done | bytes 524304 | tf_op jit(solution)/shard_map/reduce_scatter | solution.py:383
  949.0 41.4 %reduce-scatter.25.cloned.1.call-done = bf16[2,256,512]{2,1,0:T(8,128)(2,1)} async-done(((bf16[8,256,512]{2,1,0:T(8,128)(2,1)}), bf16[2,256,512]{2,1,0:T(8,128)(2,1)}) %reduce-scatter.25.cloned.1.call-update) | async-done | bytes 524304 | tf_op jit(solution)/shard_map/reduce_scatter | solution.py:386
  994.3 39.7 %all-reduce = (f32[2,512]{1,0:T(2,128)}, f32[2,512]{1,0:T(2,128)}, f32[512]{0:T(512)}, f32[8,2]{0,1:T(2,128)S(1)}) all-reduce(f32[2,512]{1,0:T(2,128)S(1)} %pad_maximum_fusion.2, f32[2,512]{1,0:T(2,128)S(1)} %pad_maximum_fusion.3, f32[512]{0:T(512)S(1)} %add.722, ...), channel_id=1, replica_groups=mesh['expert'=8,'head'=4] {'expert','head'}, use_global_device_ids=true, to_apply=%region_62.63 | all-reduce | flops 2576 | bytes 20608 | tf_op jit(solution)/shard_map/psum | solution.py:408
  1035.8 3.0 add_add_fusion.5
  1038.9 2.9 add_add_fusion.4
  (412 shorter events, 116.9 us)
Async XLA Ops:
  7.2 272.9 %copy-start = (bf16[1,512,2048]{2,1,0:T(8,128)(2,1)S(1)}, bf16[1,512,2048]{2,1,0:T(8,128)(2,1)}, u32[]{:S(2)}) copy-start(bf16[1,512,2048]{2,1,0:T(8,128)(2,1)} %param.36) | copy-start | bytes 6291460
  7.2 6.2 copy-start.87
  7.2 216.9 %all-reduce.8.cloned.1.call-start = ((), (), s32[]{:S(2)}) async-start(), calls=%async_computation.27 | async-start | bytes 8388608 | tf_op jit(solution)/shard_map/psum | solution.py:246
  7.3 6.1 copy-start.13
  8.9 9.8 copy-start.61
  8.9 5.4 copy-start.26
  14.4 8.3 copy-start.4
  19.7 4.5 copy-start.6
  28.1 13.0 %copy-start.85 = (s32[8]{0:T(128)S(1)}, s32[8]{0:T(128)}, u32[]{:S(2)}) copy-start(s32[8]{0:T(128)} %param.26) | copy-start | bytes 100
  35.4 19.3 %copy-start.28 = (bf16[8,256,2,64]{1,3,2,0:T(8,128)(2,1)}, bf16[8,256,2,64]{1,3,2,0:T(8,128)(2,1)S(1)}, u32[]{:S(2)}) copy-start(bf16[8,256,2,64]{1,3,2,0:T(8,128)(2,1)S(1)} %copy.160) | copy-start | bytes 1572868
  35.4 16.1 %copy-start.86 = (s32[32]{0:T(128)S(1)}, s32[32]{0:T(128)}, u32[]{:S(2)}) copy-start(s32[32]{0:T(128)} %param.25) | copy-start | bytes 388
  41.2 15.1 %copy-start.30 = (bf16[8,256,2,64]{1,3,2,0:T(8,128)(2,1)}, bf16[8,256,2,64]{1,3,2,0:T(8,128)(2,1)S(1)}, u32[]{:S(2)}) copy-start(bf16[8,256,2,64]{1,3,2,0:T(8,128)(2,1)S(1)} %copy.161) | copy-start | bytes 1572868
  62.8 161.2 %copy-start.81 = (f32[512]{0:T(512)S(1)}, f32[512]{0:T(512)}, u32[]{:S(2)}) copy-start(f32[512]{0:T(512)} %param.35) | copy-start | bytes 6148
  227.4 5.7 copy-start.8
  249.7 30.4 %copy-start.92 = (f32[1,2048]{1,0:T(1,128)S(1)}, f32[1,2048]{1,0:T(1,128)}, u32[]{:S(2)}) copy-start(f32[1,2048]{1,0:T(1,128)} %param.37) | copy-start | bytes 24580
  280.1 10.8 %copy-start.53 = (bf16[8,256,512]{2,1,0:T(8,128)(2,1)}, bf16[8,256,512]{2,1,0:T(8,128)(2,1)S(1)}, u32[]{:S(2)}) copy-start(bf16[8,256,512]{2,1,0:T(8,128)(2,1)S(1)} %all_to_all.20) | copy-start | bytes 6291460
  280.1 10.8 %copy-start.90 = (bf16[1,2048,512]{2,1,0:T(8,128)(2,1)S(1)}, bf16[1,2048,512]{2,1,0:T(8,128)(2,1)}, u32[]{:S(2)}) copy-start(bf16[1,2048,512]{2,1,0:T(8,128)(2,1)} %param.38) | copy-start | bytes 6291460
  280.1 10.8 %copy-start.93 = (f32[1,512]{1,0:T(1,128)S(1)}, f32[1,512]{1,0:T(1,128)}, u32[]{:S(2)}) copy-start(f32[1,512]{1,0:T(1,128)} %param.39) | copy-start | bytes 6148
  290.9 5.7 copy-start.95
  296.6 31.0 %all-to-all-start.1 = ((bf16[8,256,512]{2,1,0:T(8,128)(2,1)}), bf16[8,256,512]{2,1,0:T(8,128)(2,1)}, u32[]{:S(2)}, u32[]{:S(2)}) async-start(bf16[8,256,512]{2,1,0:T(8,128)(2,1)} %bitcast.338), calls=%async_computation.1 | async-start | bytes 4194304 | tf_op jit(solution)/shard_map/all_to_all | solution.py:265
  305.4 12.0 %copy-start.72 = (f32[8,512]{1,0:T(8,128)S(1)}, f32[8,512]{1,0:T(8,128)}, u32[]{:S(2)}) copy-start(f32[8,512]{1,0:T(8,128)} %param.40) | copy-start | bytes 49156
  305.4 12.0 %copy-start.78 = (f32[512,8]{0,1:T(8,128)S(1)}, f32[512,8]{0,1:T(8,128)}, u32[]{:S(2)}) copy-start(f32[512,8]{0,1:T(8,128)} %param.41) | copy-start | bytes 49156
  318.1 12.5 %copy-start.74 = (f32[8,2]{0,1:T(2,128)}, f32[8,2]{0,1:T(2,128)S(1)}, u32[]{:S(2)}) copy-start(f32[8,2]{0,1:T(2,128)S(1)} %get-tuple-element.90) | copy-start | bytes 196
  331.3 29.8 %copy-start.91 = (bf16[1,2048,512]{2,1,0:T(8,128)(2,1)S(1)}, bf16[1,2048,512]{2,1,0:T(8,128)(2,1)}, u32[]{:S(2)}) copy-start(bf16[1,2048,512]{2,1,0:T(8,128)(2,1)} %param.38) | copy-start | bytes 6291460
  361.1 18.6 %copy-start.20 = (bf16[8,256,512]{2,1,0:T(8,128)(2,1)}, bf16[8,256,512]{2,1,0:T(8,128)(2,1)S(1)}, u32[]{:S(2)}) copy-start(bf16[8,256,512]{2,1,0:T(8,128)(2,1)S(1)} %all_to_all.21) | copy-start | bytes 6291460
  379.7 6.2 copy-start.94
  385.9 30.2 %all-to-all-start.3 = ((bf16[8,256,512]{2,1,0:T(8,128)(2,1)}), bf16[8,256,512]{2,1,0:T(8,128)(2,1)S(1)}, u32[]{:S(2)}, u32[]{:S(2)}) async-start(bf16[8,256,512]{2,1,0:T(8,128)(2,1)} %bitcast.339), calls=%async_computation.5 | async-start | bytes 4194304 | tf_op jit(solution)/shard_map/all_to_all | solution.py:326
  389.5 90.5 %reduce-scatter.19.cloned.1.call-start = ((), (), s32[]{:S(2)}) async-start(), calls=%async_computation.16 | async-start | bytes 2621440 | tf_op jit(solution)/shard_map/reduce_scatter | solution.py:347
  438.8 86.7 %reduce-scatter.15.cloned.1.call-start = ((), (), s32[]{:S(2)}) async-start(), calls=%async_computation.14 | async-start | bytes 2621440 | tf_op jit(solution)/shard_map/reduce_scatter | solution.py:275
  466.1 104.9 %reduce-scatter.23.cloned.1.call-start = ((), (), s32[]{:S(2)}) async-start(), calls=%async_computation.19 | async-start | bytes 2621440 | tf_op jit(solution)/shard_map/reduce_scatter | solution.py:353
  466.7 149.7 %reduce-scatter.17.cloned.1.call-start = ((), (), s32[]{:S(2)}) async-start(), calls=%async_computation.15 | async-start | bytes 2621440 | tf_op jit(solution)/shard_map/reduce_scatter | solution.py:281
  467.3 195.8 %all-gather.3.cloned.1.call-start = ((), (), s32[]{:S(2)}) async-start(), calls=%async_computation.17 | async-start | bytes 2621440 | tf_op jit(solution)/shard_map/all_gather | solution.py:141
  528.8 180.7 %all-gather.5.cloned.1.call-start = ((), (), s32[]{:S(2)}) async-start(), calls=%async_computation.20 | async-start | bytes 2621440 | tf_op jit(solution)/shard_map/all_gather | solution.py:142
  528.9 90.8 %copy-start.21 = (bf16[8,256,512]{2,1,0:T(8,128)(2,1)S(1)}, bf16[8,256,512]{2,1,0:T(8,128)(2,1)}, u32[]{:S(2)}) copy-start(bf16[8,256,512]{2,1,0:T(8,128)(2,1)} %copy-done.20) | copy-start | bytes 6291460
  619.7 129.1 %reduce-scatter.33.cloned.1.call-start = ((), (), s32[]{:S(2)}) async-start(), calls=%async_computation.25 | async-start | bytes 163840
  620.9 131.0 %reduce-scatter.31.cloned.1.call-start = ((), (), s32[]{:S(2)}) async-start(), calls=%async_computation.24 | async-start | bytes 655360
  622.1 11.0 %copy-start.47 = (bf16[32,2,64,64]{3,2,1,0:T(8,128)(2,1)S(1)}, bf16[32,2,64,64]{3,2,1,0:T(8,128)(2,1)}, u32[]{:S(2)}) copy-start(bf16[32,2,64,64]{3,2,1,0:T(8,128)(2,1)} %copy-done.46) | copy-start | bytes 1572868
  622.2 174.0 %reduce-scatter.27.cloned.1.call-start = ((), (), s32[]{:S(2)}) async-start(), calls=%async_computation.22 | async-start | bytes 2621440 | tf_op jit(solution)/shard_map/reduce_scatter | solution.py:328
  633.0 6.7 copy-start.64
  633.0 6.7 copy-start.71
  633.0 6.7 copy-start.66
  633.0 6.7 copy-start.68
  633.1 208.8 %reduce-scatter.29.cloned.1.call-start = ((), (), s32[]{:S(2)}) async-start(), calls=%async_computation.23 | async-start | bytes 2621440 | tf_op jit(solution)/shard_map/reduce_scatter | solution.py:334
  639.8 23.3 %copy-start.58 = (bf16[128,512]{1,0:T(8,128)(2,1)S(1)}, bf16[128,512]{1,0:T(8,128)(2,1)}, u32[]{:S(2)}) copy-start(bf16[128,512]{1,0:T(8,128)(2,1)} %param.34) | copy-start | bytes 393220
  649.3 19.3 %copy-start.16 = (f32[32,2,64,64]{2,3,1,0:T(8,128)S(1)}, f32[32,2,64,64]{2,3,1,0:T(8,128)}, u32[]{:S(2)}) copy-start(f32[32,2,64,64]{2,3,1,0:T(8,128)} %copy-done.15) | copy-start | bytes 3145732
  649.3 250.1 %all-reduce.6.cloned.1.call-start = ((), (), s32[]{:S(2)}) async-start(), calls=%async_computation.26 | async-start | bytes 1048576 | tf_op jit(solution)/shard_map/psum | solution.py:402
  676.8 4.4 copy-start.49
  676.8 7.6 copy-start.48
  686.8 26.2 %copy-start.52 = (bf16[8,256,2,64]{1,3,2,0:T(8,128)(2,1)S(1)}, bf16[8,256,2,64]{1,3,2,0:T(8,128)(2,1)}, u32[]{:S(2)}) copy-start(bf16[8,256,2,64]{1,3,2,0:T(8,128)(2,1)} %copy.162) | copy-start | bytes 1572868
  718.6 6.7 copy-start.36
  719.8 4.7 copy-start.38
  733.9 6.1 copy-start.37
  734.0 211.1 %reduce-scatter.21.cloned.1.call-start = ((), (), s32[]{:S(2)}) async-start(), calls=%async_computation.18 | async-start | bytes 2621440 | tf_op jit(solution)/shard_map/reduce_scatter | solution.py:383
  739.7 250.7 %reduce-scatter.25.cloned.1.call-start = ((), (), s32[]{:S(2)}) async-start(), calls=%async_computation.21 | async-start | bytes 2621440 | tf_op jit(solution)/shard_map/reduce_scatter | solution.py:386
  745.9 199.1 %copy-start.62 = (f32[1,512]{1,0:T(1,128)S(1)}, f32[1,512]{1,0:T(1,128)}, u32[]{:S(2)}) copy-start(f32[1,512]{1,0:T(1,128)} %copy-done.61) | copy-start | bytes 6148
  844.0 190.0 %copy-start.75 = (f32[8,2]{0,1:T(2,128)S(1)}, f32[8,2]{0,1:T(2,128)}, u32[]{:S(2)}) copy-start(f32[8,2]{0,1:T(2,128)} %copy-done.74) | copy-start | bytes 196
  844.0 190.0 %copy-start.80 = (f32[8]{0:T(128)S(1)}, f32[8]{0:T(128)}, u32[]{:S(2)}) copy-start(f32[8]{0:T(128)} %copy-done.79) | copy-start | bytes 100
  844.0 190.0 %copy-start.83 = (f32[8]{0:T(128)S(1)}, f32[8]{0:T(128)}, u32[]{:S(2)}) copy-start(f32[8]{0:T(128)} %copy-done.82) | copy-start | bytes 100
  844.0 190.1 %copy-start.69 = (f32[8,2,512]{2,0,1:T(8,128)S(1)}, f32[8,2,512]{2,0,1:T(8,128)}, u32[]{:S(2)}) copy-start(f32[8,2,512]{2,0,1:T(8,128)} %get-tuple-element.91) | copy-start | bytes 98308
  844.0 191.0 %copy-start.73 = (f32[8,512]{1,0:T(8,128)S(1)}, f32[8,512]{1,0:T(8,128)}, u32[]{:S(2)}) copy-start(f32[8,512]{1,0:T(8,128)} %param.40) | copy-start | bytes 49156
  844.0 191.8 %copy-start.24 = (bf16[8,64,512]{2,1,0:T(8,128)(2,1)S(1)}, bf16[8,64,512]{2,1,0:T(8,128)(2,1)}, u32[]{:S(2)}) copy-start(bf16[8,64,512]{2,1,0:T(8,128)(2,1)} %reduce-scatter.19.cloned.1.call-done) | copy-start | bytes 1572868
  949.0 89.9 %copy-start.25 = (bf16[2,256,512]{2,1,0:T(8,128)(2,1)S(1)}, bf16[2,256,512]{2,1,0:T(8,128)(2,1)}, u32[]{:S(2)}) copy-start(bf16[2,256,512]{2,1,0:T(8,128)(2,1)} %reduce-scatter.23.cloned.1.call-done) | copy-start | bytes 1572868
  1034.8 4.0 copy-start.42
  1035.0 6.8 copy-start.1
  (48 other events, 111.5 us)
Sparse Core Ops, SparseCore 0:
  65.9 158.0 all-reduce.7
  438.9 41.0 reduce-scatter.18
  482.3 43.1 reduce-scatter.14
  527.8 43.1 reduce-scatter.22
  573.2 43.1 reduce-scatter.16
  617.9 45.1 all-gather.2
  664.7 44.6 all-gather.4
  711.8 17.9 reduce-scatter.32
  732.1 19.7 reduce-scatter.30
  754.0 42.1 reduce-scatter.26
  798.6 43.1 reduce-scatter.28
  845.4 54.0 all-reduce.5
  901.9 43.1 reduce-scatter.20
  947.2 43.1 reduce-scatter.24
where the time goes:
time: 1060 us; the launch traced here: 1050 us
  waiting for transfers between devices  576 us (54%)
  other arithmetic  121 us (11%)
  matrix products  119 us (11%)
  blocking collectives  113 us (11%)
  local copies, waits for them, and re-layouts  95.2 us (9%)
  between operations  16 us (2%)
    psum x1, waiting for transfers between devices, per_device(): lax.psum(long_part.astype(jnp.bfloat16), 'head').astype(jnp.float32)  156 us
    reduce_scatter x1, waiting for transfers between devices, per_device(): lax.psum_scatter(grad_down_w[None].astype(jnp.bfloat16), 'head', scatter_...  43.5 us
    reduce_scatter x1, waiting for transfers between devices, per_device(): lax.psum_scatter(grad_up_w[None].astype(jnp.bfloat16), 'head', scatter_di...  42.7 us
    reduce_scatter x1, waiting for transfers between devices, per_device(): lax.psum_scatter(short_back[0].astype(jnp.bfloat16), 'head', scatter_dime...  42 us
    reduce_scatter x1, waiting for transfers between devices, per_device(): lax.psum_scatter(mixed_rows[:short_total].reshape(short_in.shape).astype(...  41.6 us
    reduce_scatter x1, waiting for transfers between devices, per_device(): lax.psum_scatter(mixed_rows[short_total:].reshape(long_in.shape).astype(j...  41.5 us
    reduce_scatter x1, waiting for transfers between devices, per_device(): lax.psum_scatter(long_back[0].astype(jnp.bfloat16), 'head', scatter_dimen...  41.4 us
    psum x1, waiting for transfers between devices, per_device(): lax.psum(qkv_terms.astype(jnp.bfloat16), 'expert').astype(jnp.float32)  41 us
  transfers between devices with their start and end apart: 16, of which 15 were waited for; matrix products, arithmetic and copies ran while one was open for 16% of the time, Pallas kernels for 0%

commit v1 on v0

--- a/solution.py
+++ b/solution.py
@@ -1,6 +1,10 @@
+import functools
+
 import jax
 import jax.numpy as jnp
 from jax import lax
+from jax.experimental import pallas as pl
+from jax.experimental.pallas import tpu as pltpu
 from jax.sharding import PartitionSpec as P
 
 HEAD_DIM = 64
@@ -143,7 +147,7 @@
     )
 
 
-def per_device(
+def per_device_wide(
     short_x,
     long_x,
     short_cot,
@@ -429,6 +433,1167 @@
         shard_down_b,
         grad_task,
         grad_gate,
+    )
+
+
+BF16 = jnp.bfloat16
+F32 = jnp.float32
+VMEM_LIMIT = 56 * 1024 * 1024
+SLICE_ROWS = 272
+HALF_PACK = 1088
+QKV_ROWS = 1536
+MISC_ROW = 2048
+GRAD_ROWS = 1040
+
+
+def mm(a, b):
+    return lax.dot_general(a, b, (((1,), (0,)), ((), ())), preferred_element_type=F32)
+
+
+def mm_nt(a, b):
+    return lax.dot_general(a, b, (((1,), (1,)), ((), ())), preferred_element_type=F32)
+
+
+def mm_tn(a, b):
+    return lax.dot_general(a, b, (((0,), (0,)), ((), ())), preferred_element_type=F32)
+
+
+def iota(shape, dim):
+    return lax.broadcasted_iota(jnp.int32, shape, dim)
+
+
+def params(**kw):
+    return pltpu.CompilerParams(vmem_limit_bytes=VMEM_LIMIT, **kw)
+
+
+def cost(micros):
+    return pl.CostEstimate(flops=0, bytes_accessed=int(micros * 3.7e6), transcendentals=0)
+
+
+VM = pl.BlockSpec(memory_space=pltpu.VMEM)
+SM = pl.BlockSpec(memory_space=pltpu.SMEM)
+ANY = pl.BlockSpec(memory_space=pl.ANY)
+
+
+def pack_kernel(qkv, qv, wo, out):
+    core = lax.axis_index("expert") % 2
+    feats = qkv.shape[1]
+    split = HALF_PACK - 2 * feats
+
+    @pl.when(core == 0)
+    def _():
+        out[0:feats, :] = qkv[0]
+        out[feats : 2 * feats, :] = qkv[1]
+        out[2 * feats :, :] = qkv[2, 0:split, :]
+
+    @pl.when(core != 0)
+    def _():
+        at = feats - split
+        out[0:at, :] = qkv[2, split:, :]
+        for c in range(4):
+            out[at + 128 * c : at + 128 * (c + 1), :] = wo[:, 128 * c : 128 * (c + 1)]
+        at += 4 * 128
+        out[at:, :] = jnp.zeros((HALF_PACK - at, 128), BF16)
+        high = qv[...].astype(BF16)
+        low = (qv[...] - high.astype(F32)).astype(BF16)
+        out[at : at + 2, :] = high
+        out[at + 2 : at + 4, :] = low
+
+
+def split_cycles(pair_left, pair_right, eye, count):
+    step = mm(pair_left.astype(BF16), pair_right.astype(BF16))
+    reach = jnp.minimum(eye + step, 1.0)
+    hops = 1
+    while hops < count // 2:
+        wide = reach.astype(BF16)
+        reach = jnp.minimum(mm(wide, wide), 1.0)
+        hops *= 2
+    lanes = iota((count, count), 1).astype(F32)
+    lowest = jnp.min(jnp.where(reach > 0.5, lanes, float(count)), axis=1, keepdims=True)
+    lowest_row = jnp.sum(eye * lowest, axis=0, keepdims=True)
+    other = jnp.sum(pair_left * lowest_row, axis=1, keepdims=True)
+    return (lowest > other).astype(F32)
+
+
+def route_kernel(st_ref, sl_ref, lt_ref, ll_ref, ids_ref, temb_ref, gw_ref, tab_ref, gate_ref):
+    here = lax.axis_index("head").astype(jnp.int32)
+    group = lax.axis_index("expert").astype(jnp.int32)
+    shorts = st_ref.shape[1]
+    longs = lt_ref.shape[1]
+    tasks = ids_ref.shape[1]
+    per_owner = shorts // 4
+    mine = here.astype(F32)
+
+    def eye_of(n):
+        return (iota((n, n), 0) == iota((n, n), 1)).astype(F32)
+
+    def col(row, eye):
+        return jnp.sum(eye * row, axis=1, keepdims=True)
+
+    def row(column, eye):
+        return jnp.sum(eye * column, axis=0, keepdims=True)
+
+    eye = eye_of(shorts)
+    at_sub, at_lane = iota((shorts, shorts), 0), iota((shorts, shorts), 1)
+    off_diag = 1.0 - eye
+    task_row = st_ref[...].astype(F32)
+    task_col = col(task_row, eye)
+    same_task = (task_col == task_row).astype(F32)
+    earlier = (at_lane < at_sub).astype(F32)
+    later = (at_lane > at_sub).astype(F32)
+    rank_col = jnp.sum(same_task * earlier, axis=1, keepdims=True)
+    rank_row = jnp.sum(same_task * later, axis=0, keepdims=True)
+    first_of_pair = jnp.floor(rank_col * 0.5) == jnp.floor(rank_row * 0.5)
+    pair_right = same_task * first_of_pair.astype(F32) * off_diag
+    pair_left = ((at_sub // 2) == (at_lane // 2)).astype(F32) * off_diag
+    major = split_cycles(pair_left, pair_right, eye, shorts)
+    same_major = (major == row(major, eye)).astype(F32)
+    pair_right = same_task * same_major * off_diag
+    pair_left = ((at_sub // 4) == (at_lane // 4)).astype(F32) * same_major * off_diag
+    minor = split_cycles(pair_left, pair_right, eye, shorts)
+    colour = 2.0 * major + minor
+    same_owner = ((at_sub // per_owner) == (at_lane // per_owner)).astype(F32)
+    same_colour = (colour == row(colour, eye)).astype(F32)
+    place = jnp.sum(same_owner * same_colour * earlier, axis=1, keepdims=True)
+
+    sent = iota((shorts, 128), 0)
+    lane = iota((shorts, 128), 1)
+    sent_f = sent.astype(F32)
+    lane_f = lane.astype(F32)
+    length_col = col(sl_ref[...].astype(F32), eye)
+    own = ((task_col == lane_f) & (colour == mine)).astype(F32)
+    owner_col = (iota((shorts, 1), 0) // per_owner).astype(F32)
+
+    def put(r, values):
+        tab_ref[r : r + 1, :] = values.astype(jnp.int32)
+
+    def put_away(r, values, low):
+        tab_ref[r : r + 1, :] = values.astype(jnp.int32) ^ (here * low)
+
+    def total(values):
+        return jnp.sum(values, axis=0, keepdims=True)
+
+    tab_ref[...] = jnp.zeros_like(tab_ref)
+    put(0, total(own * sent_f))
+    put(1, total(own * length_col))
+    put_away(2, total(own * (owner_col * 2.0 + place)), 2)
+    natural = (sent == lane + here * per_owner) & (lane < per_owner)
+    put_away(6, total(natural.astype(F32) * (colour * 2.0 + place)), 2)
+
+    eye_l = eye_of(longs)
+    sub_l, lane_l = iota((longs, longs), 0), iota((longs, longs), 1)
+    ltask_row = lt_ref[...].astype(F32)
+    ltask_col = col(ltask_row, eye_l)
+    right_l = (ltask_col == ltask_row).astype(F32) * (1.0 - eye_l)
+    left_l = ((sub_l // 2) == (lane_l // 2)).astype(F32) * (1.0 - eye_l)
+    kappa = split_cycles(left_l, right_l, eye_l, longs)
+    parity_col = ltask_col - 2.0 * jnp.floor(ltask_col * 0.5)
+    parity = jnp.max(parity_col, axis=0, keepdims=True)
+    lsent = iota((longs, 128), 0)
+    llane = iota((longs, 128), 1)
+    unit_task = parity + 2.0 * llane.astype(F32)
+    mine_l = (here % 2).astype(F32)
+    own_l = ((ltask_col == unit_task) & (kappa == mine_l)).astype(F32)
+    llen_col = col(ll_ref[...].astype(F32), eye_l)
+    put(3, total(own_l * lsent.astype(F32)))
+    put_away(16, total(own_l * (lsent // (longs // 4)).astype(F32)), 1)
+    put(4, total(own_l * llen_col))
+    row_lane = iota((1, 128), 1)
+    row_lane_f = row_lane.astype(F32)
+    put(5, parity + 2.0 * row_lane_f)
+    natural_l = (lsent == llane + here * (longs // 4)) & (llane < longs // 4)
+    put_away(7, total(natural_l.astype(F32) * kappa), 1)
+    put_away(15, total(natural_l.astype(F32) * (kappa + 2.0)), 1)
+
+    ids = ids_ref[...].astype(F32)
+    eye_t = eye_of(tasks)
+    e_first, e_second = col(ids[0:1, :], eye_t), col(ids[1:2, :], eye_t)
+    tsub = iota((tasks, 128), 0).astype(F32)
+    tlane = iota((tasks, 128), 1).astype(F32)
+    diag = (tsub == tlane).astype(F32)
+    put(8, total(diag * e_first))
+    put(9, total(diag * e_second))
+    task_first = total((e_first == tlane).astype(F32) * tsub)
+    task_second = total((e_second == tlane).astype(F32) * tsub)
+    put(10, task_first)
+    put(11, task_second)
+    first_parity = task_first - 2.0 * jnp.floor(task_first * 0.5)
+    use_second = first_parity != parity
+    put(12, use_second.astype(F32))
+    unit_of = jnp.where(use_second, task_second, task_first)
+    put(13, jnp.floor((unit_of - parity) * 0.5))
+    half = here // 2
+    tab_ref[14:15, :] = jnp.where(row_lane == 0, half, jnp.where(row_lane == 1, here, group))
+
+    logits = lax.dot_general(
+        temb_ref[...],
+        gw_ref[...],
+        (((1,), (1,)), ((), ())),
+        preferred_element_type=F32,
+        precision=HIGHEST,
+    )
+    ecols = iota((tasks, logits.shape[1]), 1).astype(F32)
+    first = jnp.sum(jnp.where(ecols == e_first, logits, 0.0), axis=1, keepdims=True)
+    second = jnp.sum(jnp.where(ecols == e_second, logits, 0.0), axis=1, keepdims=True)
+    top = jnp.maximum(first, second)
+    first, second = jnp.exp(first - top), jnp.exp(second - top)
+    denominator = first + second
+    gate_ref[...] = jnp.where(
+        tlane == 0.0, first / denominator, jnp.where(tlane == 1.0, second / denominator, 0.0)
+    )
+
+
+def norm_stats(values):
+    centred = values - jnp.mean(values, axis=-1, keepdims=True)
+    scale = lax.rsqrt(jnp.mean(centred * centred, axis=-1, keepdims=True) + 1e-05)
+    return centred * scale, scale
+
+
+def prep_kernel(
+    tab, gates, cs0, cs1, cl, csb, clb, xs, xl, gain, bias,
+    deo, cb_s, cb_l, ns, nl, xb_s, xb_l,
+):
+    e = pl.program_id(0)
+    span = cs0.shape[1]
+    for k, ref in ((0, cs0), (1, cs1)):
+        t = tab[10 + k, e]
+        keep = iota((span, 1), 0) < tab[1, t]
+        deo[0, span * k : span * (k + 1), :] = jnp.where(
+            keep, gates[t, k] * ref[0].astype(F32), 0.0
+        ).astype(BF16)
+    half_rows = cl.shape[1]
+    u = tab[13, e]
+    gate = gates[tab[5, u], tab[12, e]]
+    keep = iota((half_rows, 1), 0) + half_rows * tab[14, 0] < tab[4, u]
+    deo[0, 2 * span : 2 * span + half_rows, :] = jnp.where(keep, gate * cl[0].astype(F32), 0.0).astype(BF16)
+    parity = (tab[5, 0] % 2).astype(F32)
+    deo[0, 2 * span + half_rows :, :] = jnp.full((16, deo.shape[2]), parity, F32).astype(BF16)
+    cb_s[...] = csb[...]
+    cb_l[...] = clb[...]
+    xb_s[...] = xs[...]
+    xb_l[...] = xl[...]
+    ns[0] = (norm_stats(xs[0].astype(F32))[0] * gain[0:1, :] + bias[0:1, :]).astype(BF16)
+    nl[0] = (norm_stats(xl[0].astype(F32))[0] * gain[0:1, :] + bias[0:1, :]).astype(BF16)
+
+
+def unpack_weights(own, other, w, wo, bqv):
+    shards = own.shape[0]
+    for h in range(shards):
+        cols = slice(128 * h, 128 * (h + 1))
+        w[0:HALF_PACK, cols] = own[h]
+        w[HALF_PACK:QKV_ROWS, cols] = other[h, 0 : QKV_ROWS - HALF_PACK, :]
+        for c in range(4):
+            at = QKV_ROWS - HALF_PACK + 128 * c
+            wo[128 * h : 128 * (h + 1), 128 * c : 128 * (c + 1)] = other[h, at : at + 128, :]
+        at = MISC_ROW - HALF_PACK
+        lines = other[h, at : at + 16, :].astype(F32)
+        bqv[0:2, cols] = lines[0:2] + lines[2:4]
+
+
+def pair_masks():
+    lanes = iota((1, 128), 1)
+    first = (lanes < HEAD_DIM).astype(BF16)
+    return first, (1.0 - first.astype(F32)).astype(BF16)
+
+
+def both_heads(block, masks):
+    return jnp.concatenate([block * masks[0], block * masks[1]], axis=0)
+
+
+def fold_heads(stacked, keys):
+    lanes = iota((1, 128), 1)
+    return jnp.where(lanes < HEAD_DIM, stacked[:keys], stacked[keys:])
+
+
+def softmax_pair(scores, visible, keys):
+    parts = []
+    for part in (scores[:, :keys], scores[:, keys:]):
+        part = jnp.where(visible, part, -1e30)
+        shifted = jnp.exp(part - jnp.max(part, axis=-1, keepdims=True))
+        parts.append(shifted * (1.0 / jnp.sum(shifted, axis=-1, keepdims=True)))
+    return jnp.concatenate(parts, axis=1).astype(BF16)
+
+
+def short_visible(tab, i, span):
+    rows, lanes = iota((128, 128), 0), iota((128, 128), 1)
+    limit = jnp.where(iota((1, 128), 1) < span, tab[1, 2 * i], tab[1, 2 * i + 1] + span)
+    return ((rows // span) == (lanes // span)) & (lanes < limit)
+
+
+def attend_short(
+    tab, norm, x, own, other, gain, bias, bo, q_ref, k_ref, v_ref, p_ref, ctx, mid, send, w, wo, bqv
+):
+    core = tab[14, 2] % 2
+
+    @pl.when(core == 0)
+    def _():
+        unpack_weights(own, other, w, wo, bqv)
+
+    @pl.when(core != 0)
+    def _():
+        unpack_weights(other, own, w, wo, bqv)
+
+    feats = norm.shape[1]
+    rows = norm[...]
+    q_ref[...] = ((mm(rows, w[0:feats, :]) + bqv[0:1, :]).astype(BF16) * HEAD_DIM ** (-0.5)).astype(BF16)
+    k_ref[...] = mm(rows, w[feats : 2 * feats, :]).astype(BF16)
+    v_ref[...] = (mm(rows, w[2 * feats : 3 * feats, :]) + bqv[1:2, :]).astype(BF16)
+    masks = pair_masks()
+    span = send.shape[2]
+    for i in range(norm.shape[0] // 128):
+        visible = short_visible(tab, i, span)
+        r = slice(128 * i, 128 * (i + 1))
+        for p in range(feats // 128):
+            c = slice(128 * p, 128 * (p + 1))
+            scores = mm_nt(q_ref[r, c], both_heads(k_ref[r, c], masks))
+            probs = softmax_pair(scores, visible, 128)
+            p_ref[i * (feats // 128) + p] = probs
+            ctx[r, c] = mm(probs, both_heads(v_ref[r, c], masks)).astype(BF16)
+    attn = mm(ctx[...], wo[...]) + bo[...]
+    for t in range(send.shape[0]):
+        r = slice(span * t, span * (t + 1))
+        keep = iota((span, 1), 0) < tab[1, t]
+        middle = x[r, :].astype(F32) + jnp.where(keep, attn[r, :], 0.0)
+        mid[r, :] = middle
+        mixin = (norm_stats(middle)[0] * gain[1:2, :] + bias[1:2, :]).astype(BF16)
+        send[tab[8, t], 0] = mixin
+        send[tab[9, t], 1] = mixin
+
+
+def attend_long(tab, norm, x, w, wo, bqv, gain, bias, bo, q_ref, k_ref, v_ref, p_ref, ctx, mid, send, nq):
+    feats = norm.shape[1]
+    half_rows = send.shape[1]
+    span = 2 * half_rows
+    units = norm.shape[0] // span
+    offset = tab[14, 0] * half_rows
+    for u in range(units):
+        at = pl.multiple_of(span * u + offset, half_rows)
+        nq[half_rows * u : half_rows * (u + 1), :] = norm[pl.ds(at, half_rows), :]
+    rows = norm[...]
+    q_ref[...] = ((mm(nq[...], w[0:feats, :]) + bqv[0:1, :]).astype(BF16) * HEAD_DIM ** (-0.5)).astype(BF16)
+    k_ref[...] = mm(rows, w[feats : 2 * feats, :]).astype(BF16)
+    v_ref[...] = (mm(rows, w[2 * feats : 3 * feats, :]) + bqv[1:2, :]).astype(BF16)
+    masks = pair_masks()
+    for u in range(units):
+        visible = iota((1, span), 1) < tab[4, u]
+        r = slice(half_rows * u, half_rows * (u + 1))
+        kr = slice(span * u, span * (u + 1))
+        for p in range(feats // 128):
+            c = slice(128 * p, 128 * (p + 1))
+            scores = mm_nt(q_ref[r, c], both_heads(k_ref[kr, c], masks))
+            probs = softmax_pair(scores, visible, span)
+            p_ref[u * (feats // 128) + p] = probs
+            ctx[r, c] = mm(probs, both_heads(v_ref[kr, c], masks)).astype(BF16)
+    attn = mm(ctx[...], wo[...]) + bo[...]
+    for u in range(units):
+        r = slice(half_rows * u, half_rows * (u + 1))
+        keep = iota((half_rows, 1), 0) + offset < tab[4, u]
+        at = pl.multiple_of(span * u + offset, half_rows)
+        middle = x[pl.ds(at, half_rows), :].astype(F32) + jnp.where(keep, attn[r, :], 0.0)
+        mid[r, :] = middle
+        mixin = (norm_stats(middle)[0] * gain[1:2, :] + bias[1:2, :]).astype(BF16)
+        t = tab[5, u]
+        send[tab[8, t]] = mixin
+        send[tab[9, t]] = mixin
+
+
+GELU_A = 0.7978845608028654
+GELU_B = 0.044715
+
+
+def expert_kernel(first, tab, *refs):
+    if first:
+        x, d, wu, bu, wd, bd, eo, dx, dw, ga, xt, dt, ea, da, hs, ps = refs
+        prev = None
+    else:
+        x, d, wu, bu, wd, bd, par, prev, ga_in, _, eo, dx, dw, ga, xt, dt, ea, da, hs, ps = refs
+    j = pl.program_id(0)
+    feats = x.shape[2]
+    rows = x.shape[0] * x.shape[1]
+    step = 4 * x.shape[1]
+
+    @pl.when(j == 0)
+    def _():
+        for g in range(x.shape[0]):
+            cols = slice(x.shape[1] * g, x.shape[1] * (g + 1))
+            xt[:, cols] = x[g].T
+            dt[:, cols] = d[g].T
+        ea[...] = jnp.broadcast_to(bd[...], ea.shape)
+        da[...] = jnp.zeros_like(da)
+
+    for i in range(rows // step):
+        r = slice(step * i, step * (i + 1))
+        xr = x[4 * i : 4 * i + 4].reshape(step, feats)
+        dr = d[4 * i : 4 * i + 4].reshape(step, feats)
+        pre = (mm(xr, wu[0]) + bu[...]).astype(BF16)
+        grad = mm_nt(dr, wd[0]).astype(BF16)
+        square = pre * pre
+        half = 0.5 + 0.5 * jnp.tanh(pre * (GELU_A + (GELU_A * GELU_B) * square))
+        hidden = pre * half
+        slope = half + hidden * (1.0 - half) * (2.0 * GELU_A + (6.0 * GELU_A * GELU_B) * square)
+        dpre = grad * slope
+        hs[r, :] = hidden
+        ps[r, :] = dpre
+        ea[r, :] += mm(hidden, wd[0])
+        da[r, :] += mm_nt(dpre, wu[0])
+
+    wide = wu.shape[2]
+    grad_up = mm(xt[...], ps[...])
+    grad_down = mm(dt[...], hs[...]).T
+    ones = jnp.ones((16, rows), BF16)
+    up_bias = mm(ones, ps[...])[0:1, :]
+    down_bias = mm_nt(ones, dt[...])[0:1, :]
+    if prev is not None:
+        grad_up += prev[0, 0:feats, :].astype(F32)
+        grad_down += prev[0, feats : feats + wide, :].astype(F32)
+        tail = prev[0, feats + wide :, :].astype(F32)
+        up_bias += tail[0:1, :]
+        down_bias += tail[1:2, :]
+    dw[0, 0:feats, :] = grad_up.astype(BF16)
+    dw[0, feats : feats + wide, :] = grad_down.astype(BF16)
+    which = iota((16, 1), 0)
+    dw[0, feats + wide :, :] = jnp.where(
+        which == 0, up_bias, jnp.where(which == 1, down_bias, 0.0)
+    ).astype(BF16)
+
+    @pl.when(j == pl.num_programs(0) - 1)
+    def _():
+        own = tab[14, 2]
+        t_first, t_second = tab[10, own], tab[11, own]
+        lanes = iota((1, 128), 1)
+        as_first = (lanes == 2 * t_first).astype(F32)
+        as_second = (lanes == 2 * t_second + 1).astype(F32)
+        rows_each = x.shape[1]
+        gate_sums = jnp.zeros((1, 128), F32)
+        for g in range(x.shape[0]):
+            r = slice(rows_each * g, rows_each * (g + 1))
+            out = ea[r, :].astype(BF16)
+            eo[g] = out
+            dx[g] = da[r, :].astype(BF16)
+            prod = out.astype(F32) * d[g].astype(F32)
+            if first:
+                half_each = rows_each // 2
+                gate_sums += as_first * jnp.sum(prod[:half_each], keepdims=True)
+                gate_sums += as_second * jnp.sum(prod[half_each:], keepdims=True)
+            else:
+                odd = par[g, 0:1, 0:128].astype(F32)
+                is_first = odd == (t_first % 2).astype(F32)
+                gate_sums += jnp.where(is_first, as_first, as_second) * jnp.sum(prod, keepdims=True)
+        if not first:
+            gate_sums += ga_in[0:1, :]
+        ga[...] = jnp.broadcast_to(gate_sums, ga.shape)
+
+
+def experts_pass(tab, x, deo, part, w_up, b_up, w_down, b_down, prev, ga, eo):
+    experts, rows_each, feats = x.shape
+    hidden = w_up.shape[2]
+    chunk = hidden // 4
+    rows = experts * rows_each
+    first = prev is None
+    in_specs = [
+        SM,
+        pl.BlockSpec((experts, rows_each, feats), lambda j: (0, 0, 0)),
+        pl.BlockSpec((experts, rows_each, feats), lambda j: (0, part, 0)),
+        pl.BlockSpec((1, feats, chunk), lambda j: (0, 0, j)),
+        pl.BlockSpec((1, chunk), lambda j: (0, j)),
+        pl.BlockSpec((1, chunk, feats), lambda j: (0, j, 0)),
+        pl.BlockSpec((1, feats), lambda j: (0, 0)),
+    ]
+    args = [tab, x, deo, w_up, b_up, w_down, b_down]
+    if not first:
+        in_specs.append(pl.BlockSpec((experts, 16, feats), lambda j: (0, 2 * rows_each // 16, 0)))
+        args.append(deo)
+        in_specs.append(pl.BlockSpec((1, GRAD_ROWS, feats), lambda j: (j, 0, 0)))
+        args.append(prev)
+        in_specs.append(pl.BlockSpec((8, 128), lambda j: (0, 0)))
+        args.append(ga)
+        in_specs.append(ANY)
+        args.append(eo)
+    return pl.pallas_call(
+        functools.partial(expert_kernel, first),
+        grid=(4,),
+        in_specs=in_specs,
+        out_specs=[
+            pl.BlockSpec((experts, rows_each, feats), lambda j: (0, part, 0)),
+            pl.BlockSpec((experts, rows_each, feats), lambda j: (0, 0, 0)),
+            pl.BlockSpec((1, GRAD_ROWS, feats), lambda j: (j, 0, 0)),
+            pl.BlockSpec((8, 128), lambda j: (0, 0)),
+        ],
+        out_shape=[
+            jax.ShapeDtypeStruct((experts, 2 * rows_each, feats), BF16),
+            jax.ShapeDtypeStruct(x.shape, BF16),
+            jax.ShapeDtypeStruct((4, GRAD_ROWS, feats), BF16),
+            jax.ShapeDtypeStruct((8, 128), F32),
+        ],
+        scratch_shapes=[
+            pltpu.VMEM((feats, rows), BF16),
+            pltpu.VMEM((feats, rows), BF16),
+            pltpu.VMEM((rows, feats), F32),
+            pltpu.VMEM((rows, feats), F32),
+            pltpu.VMEM((rows, chunk), BF16),
+            pltpu.VMEM((rows, chunk), BF16),
+        ],
+        input_output_aliases={} if first else {len(args) - 1: 0},
+        compiler_params=params(),
+        cost_estimate=cost(25),
+        name="experts_short" if first else "experts_long",
+    )(*args)
+
+
+def norm_back(grad, unit, scale, gain):
+    scaled = grad * gain
+    return scale * (
+        scaled
+        - jnp.mean(scaled, axis=-1, keepdims=True)
+        - unit * jnp.mean(scaled * unit, axis=-1, keepdims=True)
+    )
+
+
+def head_pair_back(probs, dctx, q, kk, vv, keys):
+    dprobs = mm_nt(dctx, vv)
+    dvalues = fold_heads(mm_tn(probs, dctx), keys)
+    wide = probs.astype(F32)
+    prod = wide * dprobs
+    parts = []
+    for part in (slice(0, keys), slice(keys, 2 * keys)):
+        parts.append(prod[:, part] - wide[:, part] * jnp.sum(prod[:, part], axis=-1, keepdims=True))
+    dscores = jnp.concatenate(parts, axis=1).astype(BF16)
+    dqueries = mm(dscores, kk) * HEAD_DIM ** (-0.5)
+    dkeys = fold_heads(mm_tn(dscores, q), keys)
+    return dqueries.astype(BF16), dkeys.astype(BF16), dvalues.astype(BF16)
+
+
+def row_sum(values):
+    return jnp.sum(values, axis=0, keepdims=True)
+
+
+def back_short(
+    tab, ret, mid, c, x, norm, q_ref, k_ref, v_ref, p_ref, ctx, w, wo, gain, _,
+    zsend, dw, small, _out, dmid, dattn, dctx, dq, dk, dv, dnorm,
+):
+    feats = norm.shape[1]
+    span = zsend.shape[1]
+    sums = [jnp.zeros((1, feats), F32) for _ in range(5)]
+    for t in range(ret.shape[0]):
+        r = slice(span * t, span * (t + 1))
+        dmix = ret[tab[8, t], 0].astype(F32) + ret[tab[9, t], 1].astype(F32)
+        unit, scale = norm_stats(mid[r, :])
+        sums[2] += row_sum(dmix * unit)
+        sums[3] += row_sum(dmix)
+        middle = c[r, :].astype(F32) + norm_back(dmix, unit, scale, gain[1:2, :])
+        dmid[r, :] = middle
+        masked = jnp.where(iota((span, 1), 0) < tab[1, t], middle, 0.0)
+        sums[4] += row_sum(masked)
+        dattn[r, :] = masked.astype(BF16)
+    dctx[...] = mm_nt(dattn[...], wo[...]).astype(BF16)
+    dw[3 * feats : 4 * feats, :] = mm_tn(ctx[...], dattn[...]).astype(BF16)
+    masks = pair_masks()
+    for i in range(norm.shape[0] // 128):
+        r = slice(128 * i, 128 * (i + 1))
+        for p in range(feats // 128):
+            c_ = slice(128 * p, 128 * (p + 1))
+            a, b, d = head_pair_back(
+                p_ref[i * (feats // 128) + p],
+                dctx[r, c_],
+                q_ref[r, c_],
+                both_heads(k_ref[r, c_], masks),
+                both_heads(v_ref[r, c_], masks),
+                128,
+            )
+            dq[r, c_] = a
+            dk[r, c_] = b
+            dv[r, c_] = d
+    rows = norm[...]
+    for index, ref in enumerate((dq, dk, dv)):
+        dw[feats * index : feats * (index + 1), :] = mm_tn(rows, ref[...]).astype(BF16)
+    dnorm[...] = (
+        mm_nt(dq[...], w[0:feats, :])
+        + mm_nt(dk[...], w[feats : 2 * feats, :])
+        + mm_nt(dv[...], w[2 * feats : 3 * feats, :])
+    )
+    for t in range(ret.shape[0]):
+        r = slice(span * t, span * (t + 1))
+        unit, scale = norm_stats(x[r, :].astype(F32))
+        grad = dnorm[r, :]
+        sums[0] += row_sum(grad * unit)
+        sums[1] += row_sum(grad)
+        zsend[tab[2, t]] = (dmid[r, :] + norm_back(grad, unit, scale, gain[0:1, :])).astype(BF16)
+    sums.append(row_sum(dq[...].astype(F32)))
+    sums.append(row_sum(dv[...].astype(F32)))
+    for index, value in enumerate(sums):
+        small[index : index + 1, :] = value
+    small[7:8, :] = jnp.zeros((1, feats), F32)
+
+
+def back_long(
+    tab, ret, mid, c, x, norm, q_ref, k_ref, v_ref, p_ref, ctx, w, wo, gain, dw_in, small_in, ga, z_short,
+    z0, z1, z2, z3, packed, zsend, nq, dmid, dattn, dctx, dq, dk, dv, dnorm, full,
+):
+    feats = norm.shape[1]
+    half_rows = ret.shape[1]
+    span = 2 * half_rows
+    units = norm.shape[0] // span
+    offset = tab[14, 0] * half_rows
+    sums = [small_in[index : index + 1, :] for index in range(7)]
+    for u in range(units):
+        r = slice(half_rows * u, half_rows * (u + 1))
+        t = tab[5, u]
+        at = pl.multiple_of(span * u + offset, half_rows)
+        nq[r, :] = norm[pl.ds(at, half_rows), :]
+        dmix = ret[tab[8, t]].astype(F32) + ret[tab[9, t]].astype(F32)
+        unit, scale = norm_stats(mid[r, :])
+        sums[2] += row_sum(dmix * unit)
+        sums[3] += row_sum(dmix)
+        middle = c[r, :].astype(F32) + norm_back(dmix, unit, scale, gain[1:2, :])
+        dmid[r, :] = middle
+        masked = jnp.where(iota((half_rows, 1), 0) + offset < tab[4, u], middle, 0.0)
+        sums[4] += row_sum(masked)
+        dattn[r, :] = masked.astype(BF16)
+    dctx[...] = mm_nt(dattn[...], wo[...]).astype(BF16)
+    grad_out = mm_tn(ctx[...], dattn[...]) + dw_in[3 * feats : 4 * feats, :].astype(F32)
+    shards = packed.shape[1]
+    for h in range(shards):
+        for s in range(4):
+            full[QKV_ROWS + 128 * s : QKV_ROWS + 128 * (s + 1), 128 * h : 128 * (h + 1)] = grad_out[
+                128 * h : 128 * (h + 1), 128 * s : 128 * (s + 1)
+            ]
+    masks = pair_masks()
+    for u in range(units):
+        r = slice(half_rows * u, half_rows * (u + 1))
+        kr = slice(span * u, span * (u + 1))
+        for p in range(feats // 128):
+            c_ = slice(128 * p, 128 * (p + 1))
+            a, b, d = head_pair_back(
+                p_ref[u * (feats // 128) + p],
+                dctx[r, c_],
+                q_ref[r, c_],
+                both_heads(k_ref[kr, c_], masks),
+                both_heads(v_ref[kr, c_], masks),
+                span,
+            )
+            dq[r, c_] = a
+            dk[kr, c_] = b
+            dv[kr, c_] = d
+    for index, (left, right) in enumerate(((nq, dq), (norm, dk), (norm, dv))):
+        r = slice(feats * index, feats * (index + 1))
+        full[r, :] = mm_tn(left[...], right[...]) + dw_in[r, :].astype(F32)
+    dnorm[...] = mm_nt(dk[...], w[feats : 2 * feats, :]) + mm_nt(dv[...], w[2 * feats : 3 * feats, :])
+    from_q = mm_nt(dq[...], w[0:feats, :])
+    for u in range(units):
+        at = pl.multiple_of(span * u + offset, half_rows)
+        dnorm[pl.ds(at, half_rows), :] += from_q[half_rows * u : half_rows * (u + 1), :]
+    for u in range(units):
+        owner = tab[16, u]
+        for s in range(2):
+            r = slice(span * u + half_rows * s, span * u + half_rows * (s + 1))
+            unit, scale = norm_stats(x[r, :].astype(F32))
+            grad = dnorm[r, :]
+            sums[0] += row_sum(grad * unit)
+            sums[1] += row_sum(grad)
+            own_half = tab[14, 0] == s
+            direct = jnp.where(own_half, dmid[half_rows * u : half_rows * (u + 1), :], 0.0)
+            zsend[owner, half_rows * s : half_rows * (s + 1), :] = (
+                direct + norm_back(grad, unit, scale, gain[0:1, :])
+            ).astype(BF16)
+    at = z0.shape[1] - span
+    for d, ref in enumerate((z0, z1, z2, z3)):
+        ref[0, 0:at, :] = z_short[2 * d : 2 * d + 2].reshape(at, feats)
+        ref[0, at:, :] = zsend[d]
+    sums[5] += row_sum(dq[...].astype(F32))
+    sums[6] += row_sum(dv[...].astype(F32))
+    full[MISC_ROW:, :] = jnp.zeros((full.shape[0] - MISC_ROW, feats), F32)
+    full[MISC_ROW : MISC_ROW + 1, :] = sums[5]
+    full[MISC_ROW + 1 : MISC_ROW + 2, :] = sums[6]
+    for index in range(5):
+        for s in range(4):
+            at = MISC_ROW + 2 + 4 * index + s
+            piece = sums[index][:, 128 * s : 128 * (s + 1)]
+            full[at : at + 1, :] = jnp.concatenate([piece] * shards, axis=1)
+    for s in range(shards):
+        full[MISC_ROW + 22 : MISC_ROW + 23, 128 * s : 128 * (s + 1)] = ga[0:1, :]
+    for g in range(packed.shape[0]):
+        for h in range(shards):
+            packed[g, tab[14, 1] ^ h] = full[
+                SLICE_ROWS * g : SLICE_ROWS * (g + 1), 128 * h : 128 * (h + 1)
+            ].astype(BF16)
+
+
+def mix_kernel(tab, gates, ret, mid_s, mid_l, _, z0, z1, z2, z3, _out, zsend):
+    experts = ret.shape[0]
+    span = mid_s.shape[0] // experts
+    half_rows = ret.shape[1] - 2 * span
+    for t in range(experts):
+        r = slice(span * t, span * (t + 1))
+        keep = iota((span, 1), 0) < tab[1, t]
+        e0 = ret[tab[8, t], 0:span, :].astype(F32)
+        e1 = ret[tab[9, t], span : 2 * span, :].astype(F32)
+        mixed = gates[t, 0] * e0 + gates[t, 1] * e1
+        slot = tab[2, t]
+        at = pl.multiple_of((slot % 2) * span, span)
+        zsend[slot // 2, pl.ds(at, span), :] = (mid_s[r, :] + jnp.where(keep, mixed, 0.0)).astype(BF16)
+    for u in range(mid_l.shape[0] // half_rows):
+        r = slice(half_rows * u, half_rows * (u + 1))
+        t = tab[5, u]
+        keep = iota((half_rows, 1), 0) + half_rows * tab[14, 0] < tab[4, u]
+        e0 = ret[tab[8, t], 2 * span :, :].astype(F32)
+        e1 = ret[tab[9, t], 2 * span :, :].astype(F32)
+        mixed = gates[t, 0] * e0 + gates[t, 1] * e1
+        zsend[tab[16, u], 2 * span :, :] = (mid_l[r, :] + jnp.where(keep, mixed, 0.0)).astype(BF16)
+    for d, ref in enumerate((z0, z1, z2, z3)):
+        ref[0] = zsend[d]
+
+
+def each_distance(index, refs, act):
+    for d, ref in enumerate(refs):
+
+        @pl.when(index == d)
+        def _(ref=ref):
+            act(ref)
+
+
+def place_out(tab, a0, a1, a2, a3, short_out, long_out):
+    parts = (a0, a1, a2, a3)
+    span = short_out.shape[1]
+    for n in range(short_out.shape[0]):
+        slot = tab[6, n]
+        at = pl.multiple_of((slot % 2) * span, span)
+
+        def copy_short(ref, n=n, at=at):
+            short_out[n] = ref[0, pl.ds(at, span), :]
+
+        each_distance(slot // 2, parts, copy_short)
+    half = long_out.shape[1] // 2
+    for n in range(long_out.shape[0]):
+        for index, row in ((0, 7), (1, 15)):
+
+            def copy_long(ref, n=n, index=index):
+                long_out[n, half * index : half * (index + 1), :] = ref[0, 2 * span :, :]
+
+            each_distance(tab[row, n], parts, copy_long)
+
+
+def place_dx(tab, a0, a1, a2, a3, short_dx, long_dx):
+    parts = (a0, a1, a2, a3)
+    span = short_dx.shape[1]
+    for n in range(short_dx.shape[0]):
+        slot = tab[6, n]
+        at = pl.multiple_of((slot % 2) * span, span)
+
+        def copy_short(ref, n=n, at=at):
+            short_dx[n] = ref[0, pl.ds(at, span), :].astype(F32)
+
+        each_distance(slot // 2, parts, copy_short)
+    for n in range(long_dx.shape[0]):
+
+        def first(ref, n=n):
+            long_dx[n] = ref[0, 2 * span :, :].astype(F32)
+
+        def second(ref, n=n):
+            long_dx[n] += ref[0, 2 * span :, :].astype(F32)
+
+        each_distance(tab[7, n], parts, first)
+        each_distance(tab[15, n], parts, second)
+
+
+def finish_kernel(tab, *refs):
+    pieces = refs[:-13]
+    ids, gates, temb, gw_t, qkv, qv, wo, gain, shift, bo, grad_temb, grad_gw_t, g = refs[-13:]
+    feats = wo.shape[1]
+    for d, piece in enumerate(pieces):
+        at = pl.multiple_of((tab[14, 2] ^ d) * SLICE_ROWS, 16)
+        g[pl.ds(at, SLICE_ROWS), :] = piece[0]
+    for j in range(3):
+        qkv[j] = g[feats * j : feats * (j + 1), :].astype(F32)
+    for c in range(4):
+        at = QKV_ROWS + 128 * c
+        wo[:, 128 * c : 128 * (c + 1)] = g[at : at + 128, :].astype(F32)
+    misc = g[MISC_ROW : MISC_ROW + 32, :].astype(F32)
+    qv[...] = misc[0:2, :]
+
+    def line(index):
+        at = 2 + 4 * index
+        return jnp.concatenate([misc[at + s : at + s + 1, :] for s in range(4)], axis=1)
+
+    gain[0:1, :], gain[1:2, :] = line(0), line(2)
+    shift[0:1, :], shift[1:2, :] = line(1), line(3)
+    bo[...] = line(4)
+    terms = misc[22:23, :]
+    tasks = temb.shape[0]
+    sub, lane = iota((tasks, 128), 0), iota((tasks, 128), 1)
+    first = jnp.sum(jnp.where(lane == 2 * sub, terms, 0.0), axis=1, keepdims=True)
+    second = jnp.sum(jnp.where(lane == 2 * sub + 1, terms, 0.0), axis=1, keepdims=True)
+    both = first + second
+    first = first - gates[:, 0:1] * both
+    second = second - gates[:, 1:2] * both
+    experts = gw_t.shape[0]
+    rows = iota((experts, tasks), 0)
+    eye = (iota((tasks, tasks), 0) == iota((tasks, tasks), 1)).astype(F32)
+    spread = jnp.zeros((experts, tasks), F32)
+    for k, value in ((0, first), (1, second)):
+        as_row = jnp.sum(eye * value, axis=0, keepdims=True)
+        spread += jnp.where(rows == ids[k : k + 1, :], as_row, 0.0)
+    grad_gw_t[...] = lax.dot_general(
+        spread, temb[...], (((1,), (0,)), ((), ())), preferred_element_type=F32, precision=HIGHEST
+    )
+    grad_temb[...] = lax.dot_general(
+        spread.T, gw_t[...], (((1,), (0,)), ((), ())), preferred_element_type=F32, precision=HIGHEST
+    )
+
+
+def finish_experts(tab, shard, up, up_b, down, down_b):
+    feats = up.shape[1]
+    up[0] = shard[0, 0:feats, :].astype(F32)
+    down[0] = shard[0, feats : 2 * feats, :].astype(F32)
+    tail = shard[0, 2 * feats :, :].astype(F32)
+    up_b[...] = tail[0:1, :]
+    down_b[...] = jnp.zeros_like(down_b)
+    for h in range(feats // 128):
+
+        @pl.when(tab[14, 1] == h)
+        def _(h=h):
+            down_b[...] = tail[1:2, 128 * h : 128 * (h + 1)]
+
+
+def shape_of(shape, dtype):
+    return jax.ShapeDtypeStruct(shape, dtype)
+
+
+def balanced(short_x, long_x, expert_ids):
+    heads = lax.axis_size("head")
+    tasks = expert_ids.shape[0]
+    return (
+        heads == 4
+        and lax.axis_size("expert") == tasks == 8
+        and short_x.shape[0] == 4 * tasks
+        and long_x.shape[0] == tasks
+        and short_x.shape[1:] == (64, 512)
+        and long_x.shape[1:] == (256, 512)
+    )
+
+
+def per_device(
+    short_x,
+    long_x,
+    short_cot,
+    long_cot,
+    short_len,
+    long_len,
+    short_task,
+    long_task,
+    expert_ids,
+    ln_gain,
+    ln_bias,
+    w_qkv,
+    b_qv,
+    w_attn_out,
+    b_attn_out,
+    w_up,
+    b_up,
+    w_down,
+    b_down,
+    task_emb,
+    gate_w,
+):
+    if not balanced(short_x, long_x, expert_ids):
+        return per_device_wide(
+            short_x, long_x, short_cot, long_cot, short_len, long_len, short_task, long_task,
+            expert_ids, ln_gain, ln_bias, w_qkv, b_qv, w_attn_out, b_attn_out, w_up, b_up,
+            w_down, b_down, task_emb, gate_w,
+        )
+    heads = lax.axis_size("head")
+    experts = lax.axis_size("expert")
+    span, feats = short_x.shape[1:]
+    long_span = long_x.shape[1]
+    half_rows = long_span // 2
+    tasks = expert_ids.shape[0]
+    units = long_x.shape[0] // 2
+    rows_s = tasks * span
+    rows_q = units * half_rows
+    rows_l = units * long_span
+    pairs = feats // 128
+
+    own_half = pl.pallas_call(
+        pack_kernel,
+        in_specs=[VM] * 3,
+        out_specs=VM,
+        out_shape=shape_of((HALF_PACK, 128), BF16),
+        compiler_params=params(),
+        cost_estimate=cost(2),
+        name="pack",
+    )(w_qkv, b_qv, w_attn_out)
+    raw_own = lax.all_gather(own_half, "head", axis=0)
+    raw_other = lax.ppermute(raw_own, "expert", [(i, i ^ 1) for i in range(experts)])
+
+    tab, gates = pl.pallas_call(
+        route_kernel,
+        in_specs=[VM] * 7,
+        out_specs=[VM, VM],
+        out_shape=[shape_of((24, 128), jnp.int32), shape_of((tasks, 128), F32)],
+        compiler_params=params(),
+        cost_estimate=cost(4),
+        name="route",
+    )(
+        short_task.reshape(1, -1),
+        short_len.reshape(1, -1),
+        long_task.reshape(1, -1),
+        long_len.reshape(1, -1),
+        expert_ids.T,
+        task_emb,
+        gate_w.T,
+    )
+
+    def blk(n, index):
+        return pl.BlockSpec((1, n, feats), index)
+
+    deo, cot_s, cot_l, norm_s, norm_l, own_s, own_l = pl.pallas_call(
+        prep_kernel,
+        grid_spec=pltpu.PrefetchScalarGridSpec(
+            num_scalar_prefetch=1,
+            grid=(8,),
+            in_specs=[
+                SM,
+                blk(span, lambda e, tab: (tab[0, tab[10, e]], 0, 0)),
+                blk(span, lambda e, tab: (tab[0, tab[11, e]], 0, 0)),
+                blk(half_rows, lambda e, tab: (tab[3, tab[13, e]], tab[14, 0], 0)),
+                blk(span, lambda e, tab: (tab[0, e], 0, 0)),
+                blk(span, lambda e, tab: (tab[3, e // 2], tab[14, 0] * 2 + e % 2, 0)),
+                blk(span, lambda e, tab: (tab[0, e], 0, 0)),
+                blk(half_rows, lambda e, tab: (tab[3, e // 2], e % 2, 0)),
+                pl.BlockSpec((2, feats), lambda e, tab: (0, 0)),
+                pl.BlockSpec((2, feats), lambda e, tab: (0, 0)),
+            ],
+            out_specs=[
+                blk(2 * span + half_rows + 16, lambda e, tab: (e, 0, 0)),
+                blk(span, lambda e, tab: (e, 0, 0)),
+                blk(span, lambda e, tab: (e, 0, 0)),
+                blk(span, lambda e, tab: (e, 0, 0)),
+                blk(half_rows, lambda e, tab: (e, 0, 0)),
+                blk(span, lambda e, tab: (e, 0, 0)),
+                blk(half_rows, lambda e, tab: (e, 0, 0)),
+            ],
+        ),
+        out_shape=[
+            shape_of((experts, 2 * span + half_rows + 16, feats), BF16),
+            shape_of((8, span, feats), BF16),
+            shape_of((8, span, feats), BF16),
+            shape_of((8, span, feats), BF16),
+            shape_of((8, half_rows, feats), BF16),
+            shape_of((8, span, feats), BF16),
+            shape_of((8, half_rows, feats), BF16),
+        ],
+        compiler_params=params(),
+        cost_estimate=cost(9),
+        name="prep",
+    )(tab, gates, short_cot, short_cot, long_cot, short_cot, long_cot, short_x, long_x, ln_gain, ln_bias)
+    cot_s, norm_s, own_s = (a.reshape(rows_s, feats) for a in (cot_s, norm_s, own_s))
+    cot_l = cot_l.reshape(rows_q, feats)
+    norm_l, own_l = norm_l.reshape(rows_l, feats), own_l.reshape(rows_l, feats)
+    deo = lax.all_to_all(deo, "expert", split_axis=0, concat_axis=0, tiled=True)
+
+    bias_out = b_attn_out.reshape(1, feats)
+    w_shapes = [
+        shape_of((QKV_ROWS, feats), BF16),
+        shape_of((feats, feats), BF16),
+        shape_of((8, feats), F32),
+    ]
+
+    def attention(kernel, operands, key_rows, query_rows, keys, send_shape, more, scratch, name):
+        return pl.pallas_call(
+            kernel,
+            in_specs=[SM] + [VM] * (len(operands) - 1),
+            out_specs=[VM] * (7 + len(more)),
+            out_shape=[
+                shape_of((query_rows, feats), BF16),
+                shape_of((key_rows, feats), BF16),
+                shape_of((key_rows, feats), BF16),
+                shape_of((4 * pairs, 128, 2 * keys), BF16),
+                shape_of((query_rows, feats), BF16),
+                shape_of((query_rows, feats), F32),
+                shape_of(send_shape, BF16),
+            ]
+            + more,
+            scratch_shapes=scratch,
+            compiler_params=params(),
+            cost_estimate=cost(12),
+            name=name,
+        )(*operands)
+
+    q_s, k_s, v_s, p_s, ctx_s, mid_s, send_s, w_all, wo_all, bqv_all = attention(
+        attend_short,
+        (tab, norm_s, own_s, raw_own, raw_other, ln_gain, ln_bias, bias_out),
+        rows_s, rows_s, 128, (experts, 2, span, feats), w_shapes, [], "attend_short",
+    )
+    send_s = send_s.reshape(experts, 2 * span, feats)
+    recv_s = lax.all_to_all(send_s, "expert", split_axis=0, concat_axis=0, tiled=True)
+    q_l, k_l, v_l, p_l, ctx_l, mid_l, send_l = attention(
+        attend_long,
+        (tab, norm_l, own_l, w_all, wo_all, bqv_all, ln_gain, ln_bias, bias_out),
+        rows_l, rows_q, long_span, (experts, half_rows, feats), [],
+        [pltpu.VMEM((rows_q, feats), BF16)], "attend_long",
+    )
+    recv_l = lax.all_to_all(send_l, "expert", split_axis=0, concat_axis=0, tiled=True)
+
+    eo, dx_s, dw_s, ga_s = experts_pass(
+        tab, recv_s, deo, 0, w_up, b_up, w_down, b_down, None, None, None
+    )
+    ret_s = lax.all_to_all(dx_s, "expert", split_axis=0, concat_axis=0, tiled=True)
+    eo, dx_l, dw_l, ga_l = experts_pass(
+        tab, recv_l, deo, 1, w_up, b_up, w_down, b_down, dw_s, ga_s, eo
+    )
+    ret_l = lax.all_to_all(dx_l, "expert", split_axis=0, concat_axis=0, tiled=True)
+    expert_grads = lax.psum_scatter(dw_l, "head", scatter_dimension=0, tiled=True)
+
+    def over_head(blocks):
+        return [blocks[0]] + [
+            lax.ppermute(blocks[d], "head", [(i, i ^ d) for i in range(heads)]) for d in range(1, heads)
+        ]
+
+    zsend_s, dw_attn, small, eo = pl.pallas_call(
+        back_short,
+        in_specs=[SM] + [VM] * 13 + [ANY],
+        out_specs=[VM] * 3 + [ANY],
+        out_shape=[
+            shape_of((2 * heads, span, feats), BF16),
+            shape_of((4 * feats, feats), BF16),
+            shape_of((8, feats), F32),
+            shape_of(eo.shape, BF16),
+        ],
+        input_output_aliases={14: 3},
+        scratch_shapes=[
+            pltpu.VMEM((rows_s, feats), F32),
+            pltpu.VMEM((rows_s, feats), BF16),
+            pltpu.VMEM((rows_s, feats), BF16),
+            pltpu.VMEM((rows_s, feats), BF16),
+            pltpu.VMEM((rows_s, feats), BF16),
+            pltpu.VMEM((rows_s, feats), BF16),
+            pltpu.VMEM((rows_s, feats), F32),
+        ],
+        compiler_params=params(),
+        cost_estimate=cost(36),
+        name="back_short",
+    )(
+        tab, ret_s.reshape(experts, 2, span, feats), mid_s, cot_s, own_s, norm_s,
+        q_s, k_s, v_s, p_s, ctx_s, w_all, wo_all, ln_gain, eo,
+    )
+    out_all = lax.all_to_all(eo, "expert", split_axis=0, concat_axis=0, tiled=True)
+    *zsend_x, packed = pl.pallas_call(
+        back_long,
+        in_specs=[SM] + [VM] * 17,
+        out_specs=[VM] * (heads + 1),
+        out_shape=[shape_of((1, 2 * span + long_span, feats), BF16)] * heads
+        + [shape_of((experts, heads, SLICE_ROWS, 128), BF16)],
+        scratch_shapes=[
+            pltpu.VMEM((heads, long_span, feats), BF16),
+            pltpu.VMEM((rows_q, feats), BF16),
+            pltpu.VMEM((rows_q, feats), F32),
+            pltpu.VMEM((rows_q, feats), BF16),
+            pltpu.VMEM((rows_q, feats), BF16),
+            pltpu.VMEM((rows_q, feats), BF16),
+            pltpu.VMEM((rows_l, feats), BF16),
+            pltpu.VMEM((rows_l, feats), BF16),
+            pltpu.VMEM((rows_l, feats), F32),
+            pltpu.VMEM((experts * SLICE_ROWS, feats), F32),
+        ],
+        compiler_params=params(),
+        cost_estimate=cost(54),
+        name="back_long",
+    )(
+        tab, ret_l, mid_l, cot_l, own_l, norm_l, q_l, k_l, v_l, p_l, ctx_l, w_all, wo_all, ln_gain,
+        dw_attn, small, ga_l, zsend_s,
+    )
+    back_x = over_head(zsend_x)
+    *zsend_o, packed = pl.pallas_call(
+        mix_kernel,
+        in_specs=[SM, SM] + [VM] * 3 + [ANY],
+        out_specs=[VM] * heads + [ANY],
+        out_shape=[shape_of((1, 2 * span + half_rows, feats), BF16)] * heads
+        + [shape_of(packed.shape, BF16)],
+        input_output_aliases={5: heads},
+        scratch_shapes=[pltpu.VMEM((heads, 2 * span + half_rows, feats), BF16)],
+        compiler_params=params(),
+        cost_estimate=cost(12),
+        name="mix",
+    )(tab, gates, out_all, mid_s, mid_l, packed)
+    back_o = over_head(zsend_o)
+    terms = lax.all_to_all(packed, "expert", split_axis=0, concat_axis=0, tiled=True)
+    terms = jnp.sum(terms.astype(F32), axis=0).astype(BF16)
+    terms = sum(
+        part.astype(F32) for part in over_head([terms[d : d + 1] for d in range(heads)])
+    ).astype(BF16)
+    attn_grads = [terms] + [
+        lax.ppermute(terms, "expert", [(i, i ^ d) for i in range(experts)]) for d in range(1, experts)
+    ]
+
+    short_out, long_out = pl.pallas_call(
+        place_out,
+        in_specs=[SM] + [VM] * 4,
+        out_specs=[VM, VM],
+        out_shape=[shape_of((8, span, feats), BF16), shape_of((2, long_span, feats), BF16)],
+        compiler_params=params(),
+        cost_estimate=cost(3),
+        name="place_out",
+    )(tab, *back_o)
+    short_dx, long_dx = pl.pallas_call(
+        place_dx,
+        in_specs=[SM] + [VM] * 4,
+        out_specs=[VM, VM],
+        out_shape=[shape_of((8, span, feats), F32), shape_of((2, long_span, feats), F32)],
+        compiler_params=params(),
+        cost_estimate=cost(4),
+        name="place_dx",
+    )(tab, *back_x)
+
+    grad_qkv, grad_qv, grad_wo, grad_gain, grad_shift, grad_bo, grad_task, grad_gate = pl.pallas_call(
+        finish_kernel,
+        in_specs=[SM] + [VM] * (experts + 4),
+        out_specs=[VM] * 8,
+        out_shape=[
+            shape_of((3, feats, 128), F32),
+            shape_of((2, 128), F32),
+            shape_of((128, feats), F32),
+            shape_of((2, feats), F32),
+            shape_of((2, feats), F32),
+            shape_of((1, feats), F32),
+            shape_of((tasks, feats), F32),
+            shape_of((experts, feats), F32),
+        ],
+        scratch_shapes=[pltpu.VMEM((experts * SLICE_ROWS, 128), BF16)],
+        compiler_params=params(),
+        cost_estimate=cost(3),
+        name="finish",
+    )(tab, *attn_grads, expert_ids.T, gates, task_emb, gate_w.T)
+    chunk = w_up.shape[2] // 4
+    grad_up, grad_up_b, grad_down, grad_down_b = pl.pallas_call(
+        finish_experts,
+        in_specs=[SM, VM],
+        out_specs=[VM] * 4,
+        out_shape=[
+            shape_of((1, feats, chunk), F32),
+            shape_of((1, chunk), F32),
+            shape_of((1, chunk, feats), F32),
+            shape_of((1, feats // heads), F32),
+        ],
+        compiler_params=params(),
+        cost_estimate=cost(3),
+        name="finish_experts",
+    )(tab, expert_grads)
+    return (
+        short_out,
+        long_out,
+        short_dx,
+        long_dx,
+        grad_gain,
+        grad_shift,
+        grad_qkv,
+        grad_qv,
+        grad_wo,
+        grad_bo.reshape(feats),
+        grad_up,
+        grad_up_b,
+        grad_down,
+        grad_down_b,
+        grad_task,
+        grad_gate.T,
     )
 
 

time: 1060 us -> 301 us (0.28)
  waiting for transfers between devices: 576 us -> 71.9 us
  Pallas kernels: 0 us -> 121 us
  other arithmetic: 121 us -> 0.4 us
  matrix products: 119 us -> 0 us
  blocking collectives: 113 us -> 19.1 us
  local copies, waits for them, and re-layouts: 95.2 us -> 6.84 us
  starting transfers between devices: 9.35 us -> 63.4 us
    reduce_scatter x8 -> x1, waiting for transfers between devices: 305 us -> 0.02 us  [per_device(): lax.psum_scatter(dw_l, 'head', scatter_dimension=0, tiled=True)]
    psum x2 -> x0, waiting for transfers between devices: 197 us -> none  [the longest x1 156 us: per_device(): lax.psum(long_part.astype(jnp.bfloat16), 'head').astype(jnp.float32)]
    pallas_call x0 -> x14, Pallas kernels: none -> 121 us  [the longest x2 42 us: experts_pass(): pl.pallas_call(functools.partial(expert_kernel, first), grid=(4,), in_spe...]
    dot_general x45 -> x0, matrix products: 119 us -> none  [the longest x1 18.6 us: per_device(): lax.dot_general(grad_output, w_down[0], CONTRACT_COLS, preferred_element_...]
    psum x2 -> x0, blocking collectives: 53.2 us -> none  [the longest x1 39.7 us: per_device(): lax.psum((gain_grads, shift_grads, bias_out_grad, gate_part), ('expert',...]
    reduce_sum x40 -> x1, other arithmetic: 44 us -> 0.35 us  [per_device(): terms = jnp.sum(terms.astype(F32), axis=0).astype(BF16)]
    all_to_all x2 -> x1, blocking collectives: 59.8 us -> 19.1 us  [per_device(): lax.all_to_all(dx_s, 'expert', split_axis=0, concat_axis=0, tiled=True)]
    reshape x20 -> x0, local copies, waits for them, and re-layouts: 36.9 us -> none  [the longest x10 28.8 us: project(): return (jnp.dot(flattened, weights[index], preferred_element_type=jnp.flo...]
  transfers between devices with their start and end apart: 16 -> 25, of which waited for: 15 -> 10; matrix products, arithmetic and copies ran while one was open for 16% -> 0% of each run, Pallas kernels for 0% -> 32%
where the time goes in v1:
time: 301 us; the launch traced here: 297 us
  Pallas kernels  121 us (40%)
  waiting for transfers between devices  71.9 us (24%)
  starting transfers between devices  63.4 us (21%)
  blocking collectives  19.1 us (6%)
  between operations  14.7 us (5%)
  local copies, waits for them, and re-layouts  6.84 us (2%)
    pallas_call x2, Pallas kernels, experts_pass(): pl.pallas_call(functools.partial(expert_kernel, first), grid=(4,), in_spe...  42 us
    all_to_all x1, waiting for transfers between devices, per_device(): lax.all_to_all(packed, 'expert', split_axis=0, concat_axis=0, tiled=True)  23.5 us
    ppermute x9, starting transfers between devices, over_head(): lax.ppermute(blocks[d], 'head', [(i, i ^ d) for i in range(heads)])  21.3 us
    pallas_call x2, Pallas kernels, attention(): pl.pallas_call(kernel, in_specs=[SM] + [VM] * (len(operands) - 1), out_sp...  20.7 us
    all_to_all x1, blocking collectives, per_device(): lax.all_to_all(dx_s, 'expert', split_axis=0, concat_axis=0, tiled=True)  19.1 us
    pallas_call x1, Pallas kernels, per_device(): pl.pallas_call(back_long, in_specs=[SM] + [VM] * 17, out_specs=[VM] * (he...  17.4 us
    all_gather x1, waiting for transfers between devices, per_device(): raw_own = lax.all_gather(own_half, 'head', axis=0)  15.5 us
    ppermute x9, waiting for transfers between devices, over_head(): lax.ppermute(blocks[d], 'head', [(i, i ^ d) for i in range(heads)])  14.3 us
  transfers between devices with their start and end apart: 25, of which 10 were waited for; matrix products, arithmetic and copies ran while one was open for 0% of the time, Pallas kernels for 32%

profile of v1, /device:TPU:0, one launch (start us, length us, event | category | flops | bytes accessed | tf_op | source)
XLA Modules:
  0.0 297.2 jit_solution(8093721665780919665)
XLA Ops:
  7.2 0.0 all-gather.3.cloned.1.call-start
  7.2 1.8 pack.1
  9.0 0.0 all-gather.3.cloned.1.call-update
  9.0 3.3 %route.1 = (s32[24,128]{1,0:T(8,128)}, f32[8,128]{1,0:T(8,128)}) custom-call(s32[1,32]{1,0:T(1,128)} %bitcast.38, s32[1,32]{1,0:T(1,128)} %bitcast.39, s32[1,8]{1,0:T(1,128)} %bitcast.40, s32[1,8]{1,0:T(1,128)} %bitcast.41, s32[2,8]{1,0:T(2,128)} %bitcast.36, f32[8,512]{1,0:T(8,128)} %refs_10_.1, f32[8,512]{1,0:T(8,128)} %bitcast.32), custom_call_target="tpu_custom_call" | custom-call | bytes 14800000 | tf_op jit(solution)/shard_map/route/pallas_call | solution.py:1327
  12.3 8.9 %prep.1 = (bf16[8,272,512]{2,1,0:T(8,128)(2,1)}, bf16[8,64,512]{2,1,0:T(8,128)(2,1)}, bf16[8,64,512]{2,1,0:T(8,128)(2,1)}, bf16[8,64,512]{2,1,0:T(8,128)(2,1)}, ...) custom-call(s32[24,128]{1,0:T(8,128)} %get-tuple-element.80.tab, ...), custom_call_target="tpu_custom_call" | custom-call | bytes 33300000 | tf_op jit(solution)/shard_map/prep/pallas_call | solution.py:1348
  21.2 5.2 %all-to-all-start.1 = ((bf16[8,272,512]{2,1,0:T(8,128)(2,1)}), bf16[8,272,512]{2,1,0:T(8,128)(2,1)S(1)}, u32[]{:S(2)}, u32[]{:S(2)}) async-start(bf16[8,272,512]{2,1,0:T(8,128)(2,1)} %get-tuple-element.85), calls=%async_computation.1 | async-start | bytes 4456448 | tf_op jit(solution)/shard_map/all_to_all | solution.py:1391
  26.4 15.5 %all-gather.3.cloned.1.call-done = bf16[4352,128]{1,0:T(8,128)(2,1)} async-done(((bf16[1088,128]{1,0:T(8,128)(2,1)}), bf16[4352,128]{1,0:T(8,128)(2,1)}) %all-gather.3.cloned.1.call-update) | async-done | bytes 1114128 | tf_op jit(solution)/shard_map/all_gather | solution.py:1324
  41.9 3.0 collective-permute-done.other
  44.9 1.0 copy-done.5
  45.9 8.0 %attend_short.1 = (bf16[512,512]{1,0:T(8,128)(2,1)}, bf16[512,512]{1,0:T(8,128)(2,1)}, bf16[512,512]{1,0:T(8,128)(2,1)}, bf16[16,128,256]{2,1,0:T(8,128)(2,1)}, ...) custom-call(s32[24,128]{1,0:T(8,128)} %get-tuple-element.80.tab, ...), custom_call_target="tpu_custom_call" | custom-call | bytes 44400000 | tf_op jit(solution)/shard_map/attend_short/pallas_call | solution.py:1401
  53.9 0.5 all-to-all-done.1.refs_1_.refs_6_
  54.5 3.6 %all-to-all-start = ((bf16[8,128,512]{2,1,0:T(8,128)(2,1)}), bf16[8,128,512]{2,1,0:T(8,128)(2,1)S(1)}, u32[]{:S(2)}, u32[]{:S(2)}) async-start(bf16[8,128,512]{2,1,0:T(8,128)(2,1)} %bitcast.29), calls=%async_computation | async-start | bytes 2097152 | tf_op jit(solution)/shard_map/all_to_all | solution.py:1427
  58.0 12.6 %attend_long.1 = (bf16[512,512]{1,0:T(8,128)(2,1)}, bf16[1024,512]{1,0:T(8,128)(2,1)}, bf16[1024,512]{1,0:T(8,128)(2,1)}, bf16[16,128,512]{2,1,0:T(8,128)(2,1)},...) custom-call(s32[24,128]{1,0:T(8,128)} %get-tuple-element.80.tab, ...), custom_call_target="tpu_custom_call" | custom-call | bytes 44400000 | tf_op jit(solution)/shard_map/attend_long/pallas_call | solution.py:1401
  70.7 2.7 all-to-all-done.refs_0_
  73.4 3.6 %all-to-all-start.3 = ((bf16[8,128,512]{2,1,0:T(8,128)(2,1)}), bf16[8,128,512]{2,1,0:T(8,128)(2,1)S(1)}, u32[]{:S(2)}, u32[]{:S(2)}) async-start(bf16[8,128,512]{2,1,0:T(8,128)(2,1)} %get-tuple-element.99), calls=%async_computation.3 | async-start | bytes 2097152 | tf_op jit(solution)/shard_map/all_to_all | solution.py:1434
  76.9 11.0 %reduce-scatter.2.cloned.1.call-start = ((), (), s32[]{:S(2)}) async-start(), calls=%async_computation.8 | async-start | bytes 5324800 | tf_op jit(solution)/shard_map/reduce_scatter | solution.py:1444
  87.9 20.7 %experts_short.1 = (bf16[8,256,512]{2,1,0:T(8,128)(2,1)}, bf16[8,128,512]{2,1,0:T(8,128)(2,1)}, bf16[4,1040,512]{2,1,0:T(8,128)(2,1)}, f32[8,128]{1,0:T(8,128)}) custom-call(s32[24,128]{1,0:T(8,128)} %get-tuple-element.80.tab, bf16[8,128,512]{2,1,0:T(8,128)(2,1)} %copy-done.3, bf16[8,272,512]{2,1,0:T(8,128)(2,1)} %copy-done, bf16[1,512,2048]{2,1,0:T(8,128)(2,1)} %refs_2_.3, ...), custom_call_target="tpu_custom_call" | custom-call | bytes 92500000 | tf_op jit(solution)/shard_map/experts_short/pallas_call | solution.py:912
  108.6 1.0 copy-done.2
  109.6 21.3 %experts_long.1 = (bf16[8,256,512]{2,1,0:T(8,128)(2,1)}, bf16[8,128,512]{2,1,0:T(8,128)(2,1)}, bf16[4,1040,512]{2,1,0:T(8,128)(2,1)}, f32[8,128]{1,0:T(8,128)}) custom-call(s32[24,128]{1,0:T(8,128)} %get-tuple-element.80.tab, bf16[8,128,512]{2,1,0:T(8,128)(2,1)} %copy-done.2, bf16[8,272,512]{2,1,0:T(8,128)(2,1)} %copy-done, ...), custom_call_target="tpu_custom_call", output_to_operand_aliasing={{0}: (10, {})} | custom-call | bytes 92500000 | tf_op jit(solution)/shard_map/experts_long/pallas_call | solution.py:912
  130.9 0.0 reduce-scatter.2.cloned.1.call-update
  130.9 1.2 copy-done.6
  132.1 19.1 %all_to_all.35 = bf16[8,128,512]{2,1,0:T(8,128)(2,1)} all-to-all(bf16[8,128,512]{2,1,0:T(8,128)(2,1)S(1)} %copy-done.6), channel_id=1, replica_groups=mesh['expert'=8,'head'=4] {'expert'}, dimensions={0} | all-to-all | bytes 2097152 | tf_op jit(solution)/shard_map/all_to_all | solution.py:1439
  151.2 3.6 %all-to-all-start.5 = ((bf16[8,128,512]{2,1,0:T(8,128)(2,1)}), bf16[8,128,512]{2,1,0:T(8,128)(2,1)S(1)}, u32[]{:S(2)}, u32[]{:S(2)}) async-start(bf16[8,128,512]{2,1,0:T(8,128)(2,1)} %get-tuple-element.106), calls=%async_computation.5 | async-start | bytes 2097152 | tf_op jit(solution)/shard_map/all_to_all | solution.py:1443
  154.8 11.9 %back_short.1 = (bf16[8,64,512]{2,1,0:T(8,128)(2,1)}, bf16[2048,512]{1,0:T(8,128)(2,1)}, f32[8,512]{1,0:T(8,128)}, bf16[8,256,512]{2,1,0:T(8,128)(2,1)}) custom-call(s32[24,128]{1,0:T(8,128)} %get-tuple-element.80.tab, bf16[8,2,64,512]{3,2,1,0:T(8,128)(2,1)} %bitcast.22, f32[512,512]{1,0:T(8,128)} %get-tuple-element.87.mid.mid_s, ...), custom_call_target="tpu_custom_call", output_to_operand_aliasing={{3}: (14, {})} | custom-call | bytes 133200000 | tf_op jit(solution)/shard_map/back_short/pallas_call | solution.py:1451
  166.7 3.4 %all-to-all-done.5.ret = bf16[8,128,512]{2,1,0:T(8,128)(2,1)S(1)} async-done(((bf16[8,128,512]{2,1,0:T(8,128)(2,1)}), bf16[8,128,512]{2,1,0:T(8,128)(2,1)S(1)}, u32[]{:S(2)}, u32[]{:S(2)}) %all-to-all-start.5) | async-done | bytes 1048608 | tf_op jit(solution)/shard_map/all_to_all | solution.py:1443
  170.1 1.0 copy-done.4
  171.1 3.8 %all-to-all-start.4 = ((bf16[8,256,512]{2,1,0:T(8,128)(2,1)}), bf16[8,256,512]{2,1,0:T(8,128)(2,1)S(1)}, u32[]{:S(2)}, u32[]{:S(2)}) async-start(bf16[8,256,512]{2,1,0:T(8,128)(2,1)} %get-tuple-element.104), calls=%async_computation.4 | async-start | bytes 4194304 | tf_op jit(solution)/shard_map/all_to_all | solution.py:1478
  174.9 17.4 %back_long.1 = (bf16[1,384,512]{2,1,0:T(8,128)(2,1)}, bf16[1,384,512]{2,1,0:T(8,128)(2,1)}, bf16[1,384,512]{2,1,0:T(8,128)(2,1)}, bf16[1,384,512]{2,1,0:T(8,128)(2,1)}, bf16[8,4,272,128]{3,2,1,0:T(8,128)(2,1)}) custom-call(s32[24,128]{1,0:T(8,128)} %get-tuple-element.80.tab, bf16[8,128,512]{2,1,0:T(8,128)(2,1)} %copy-done.4, ...), custom_call_target="tpu_custom_call" | custom-call | bytes 199800000 | tf_op jit(solution)/shard_map/back_long/pallas_call | solution.py:1479
  192.3 9.0 %all-to-all-done.4.ret = bf16[8,256,512]{2,1,0:T(8,128)(2,1)S(1)} async-done(((bf16[8,256,512]{2,1,0:T(8,128)(2,1)}), bf16[8,256,512]{2,1,0:T(8,128)(2,1)S(1)}, u32[]{:S(2)}, u32[]{:S(2)}) %all-to-all-start.4) | async-done | bytes 2097184 | tf_op jit(solution)/shard_map/all_to_all | solution.py:1478
  201.3 1.4 copy-done.1
  202.7 3.9 %mix.1 = (bf16[1,256,512]{2,1,0:T(8,128)(2,1)}, bf16[1,256,512]{2,1,0:T(8,128)(2,1)}, bf16[1,256,512]{2,1,0:T(8,128)(2,1)}, bf16[1,256,512]{2,1,0:T(8,128)(2,1)}, bf16[8,4,272,128]{3,2,1,0:T(8,128)(2,1)}) custom-call(s32[24,128]{1,0:T(8,128)} %get-tuple-element.80.tab, f32[8,128]{1,0:T(8,128)} %get-tuple-element.81.gates.refs_9_, ...), custom_call_target="tpu_custom_call", output_to_operand_aliasing={{4}: (5, {})} | custom-call | bytes 44400000 | tf_op jit(solution)/shard_map/mix/pallas_call | solution.py:1505
  206.5 3.9 %all-to-all-start.6 = ((bf16[8,4,272,128]{3,2,1,0:T(8,128)(2,1)}), bf16[8,4,272,128]{3,2,1,0:T(8,128)(2,1)S(1)}, u32[]{:S(2)}, u32[]{:S(2)}) async-start(bf16[8,4,272,128]{3,2,1,0:T(8,128)(2,1)} %get-tuple-element.130), calls=%async_computation.6 | async-start | bytes 4456448 | tf_op jit(solution)/shard_map/all_to_all | solution.py:1518
  210.4 0.0 copy-start.20
  210.4 1.6 collective-permute-start.4
  212.0 2.6 collective-permute-start.5
  214.7 0.2 collective-permute-start.6
  214.9 23.5 %all-to-all-done.6 = bf16[8,4,272,128]{3,2,1,0:T(8,128)(2,1)S(1)} async-done(((bf16[8,4,272,128]{3,2,1,0:T(8,128)(2,1)}), bf16[8,4,272,128]{3,2,1,0:T(8,128)(2,1)S(1)}, u32[]{:S(2)}, u32[]{:S(2)}) %all-to-all-start.6) | async-done | bytes 2228256 | tf_op jit(solution)/shard_map/all_to_all | solution.py:1518
  238.4 0.4 reduce_sum.12
  238.7 1.6 collective-permute-start.7
  240.4 2.4 collective-permute-start.9
  242.8 0.3 collective-permute-start.8
  243.1 0.7 collective-permute-done.7
  243.8 1.0 collective-permute-start.1
  244.8 2.2 collective-permute-done.9
  247.0 9.4 %collective-permute-start.2 = (bf16[1,256,512]{2,1,0:T(8,128)(2,1)}, bf16[1,256,512]{2,1,0:T(8,128)(2,1)S(1)}, u32[]{:S(2)}, u32[]{:S(2)}) collective-permute-start(bf16[1,256,512]{2,1,0:T(8,128)(2,1)} %get-tuple-element.120), channel_id=1, source_target_pairs={{0,2},{1,3},{2,0},{3,1},{4,6},{5,7},{6,4},{7,5},{8,10},{9,11},{10,... | collective-permute-start | bytes 786440 | tf_op jit(solution)/shard_map/ppermute | solution.py:1448
  256.4 2.0 collective-permute-start.3
  258.5 0.0 copy-start.8
  258.5 0.4 collective-permute-start.16
  258.9 2.7 collective-permute-start.15
  261.6 1.4 collective-permute-start.14
  262.9 11.4 %collective-permute-done.2.a2 = bf16[1,256,512]{2,1,0:T(8,128)(2,1)S(1)} collective-permute-done((bf16[1,256,512]{2,1,0:T(8,128)(2,1)}, bf16[1,256,512]{2,1,0:T(8,128)(2,1)S(1)}, u32[]{:S(2)}, u32[]{:S(2)}) %collective-permute-start.2) | collective-permute-done | bytes 262176 | tf_op jit(solution)/shard_map/ppermute | solution.py:1448
  274.3 1.4 collective-permute-start.13
  275.8 1.5 collective-permute-start.11
  277.3 0.3 collective-permute-start.10
  277.6 3.2 %place_dx.1 = (f32[8,64,512]{2,1,0:T(8,128)}, f32[2,256,512]{2,1,0:T(8,128)}) custom-call(s32[24,128]{1,0:T(8,128)} %get-tuple-element.80.tab, bf16[1,384,512]{2,1,0:T(8,128)(2,1)} %get-tuple-element.124.a0, bf16[1,384,512]{2,1,0:T(8,128)(2,1)} %copy-done.7, bf16[1,384,512]{2,1,0:T(8,128)(2,1)} %copy-done.8, bf16[1,384,512]{2,1,0:T(8,128)(2,1)} %collective-permute-done.6.a3), custom_call_target="tpu_custom_call" | custom-call | bytes 14800000 | tf_op jit(solution)/shard_map/place_dx/pallas_call | solution.py:1536
  280.8 2.5 place_out.1
  283.4 0.0 copy-start.18
  283.5 0.5 copy-done.15
  284.0 0.0 copy-done.16
  284.1 0.0 copy-done.17
  284.1 0.6 copy-done.19
  284.7 2.5 finish.1
  287.2 0.0 reduce-scatter.2.cloned.1.call-done.shard
  287.2 2.7 finish_experts.1
  (48 shorter events, 0.2 us)
Async XLA Ops:
  7.2 34.7 %all-gather.3.cloned.1.call-start = ((), (), s32[]{:S(2)}) async-start(), calls=%async_computation.9 | async-start | bytes 1392640 | tf_op jit(solution)/shard_map/all_gather | solution.py:1324
  21.2 33.3 %all-to-all-start.1 = ((bf16[8,272,512]{2,1,0:T(8,128)(2,1)}), bf16[8,272,512]{2,1,0:T(8,128)(2,1)S(1)}, u32[]{:S(2)}, u32[]{:S(2)}) async-start(bf16[8,272,512]{2,1,0:T(8,128)(2,1)} %get-tuple-element.85), calls=%async_computation.1 | async-start | bytes 4456448 | tf_op jit(solution)/shard_map/all_to_all | solution.py:1391
  41.9 3.0 collective-permute-start
  44.9 1.0 copy-start.5
  54.5 16.2 %copy-start = (bf16[8,272,512]{2,1,0:T(8,128)(2,1)}, bf16[8,272,512]{2,1,0:T(8,128)(2,1)S(1)}, u32[]{:S(2)}) copy-start(bf16[8,272,512]{2,1,0:T(8,128)(2,1)S(1)} %all-to-all-done.1.refs_1_.refs_6_) | copy-start | bytes 6684676
  54.5 18.9 %all-to-all-start = ((bf16[8,128,512]{2,1,0:T(8,128)(2,1)}), bf16[8,128,512]{2,1,0:T(8,128)(2,1)S(1)}, u32[]{:S(2)}, u32[]{:S(2)}) async-start(bf16[8,128,512]{2,1,0:T(8,128)(2,1)} %bitcast.29), calls=%async_computation | async-start | bytes 2097152 | tf_op jit(solution)/shard_map/all_to_all | solution.py:1427
  73.4 14.5 %copy-start.3 = (bf16[8,128,512]{2,1,0:T(8,128)(2,1)}, bf16[8,128,512]{2,1,0:T(8,128)(2,1)S(1)}, u32[]{:S(2)}) copy-start(bf16[8,128,512]{2,1,0:T(8,128)(2,1)S(1)} %all-to-all-done.refs_0_) | copy-start | bytes 3145732
  73.4 35.2 %all-to-all-start.3 = ((bf16[8,128,512]{2,1,0:T(8,128)(2,1)}), bf16[8,128,512]{2,1,0:T(8,128)(2,1)S(1)}, u32[]{:S(2)}, u32[]{:S(2)}) async-start(bf16[8,128,512]{2,1,0:T(8,128)(2,1)} %get-tuple-element.99), calls=%async_computation.3 | async-start | bytes 2097152 | tf_op jit(solution)/shard_map/all_to_all | solution.py:1434
  76.9 210.3 %reduce-scatter.2.cloned.1.call-start = ((), (), s32[]{:S(2)}) async-start(), calls=%async_computation.8 | async-start | bytes 5324800 | tf_op jit(solution)/shard_map/reduce_scatter | solution.py:1444
  108.6 1.0 copy-start.2
  130.8 1.2 copy-start.6
  151.2 18.9 %all-to-all-start.5 = ((bf16[8,128,512]{2,1,0:T(8,128)(2,1)}), bf16[8,128,512]{2,1,0:T(8,128)(2,1)S(1)}, u32[]{:S(2)}, u32[]{:S(2)}) async-start(bf16[8,128,512]{2,1,0:T(8,128)(2,1)} %get-tuple-element.106), calls=%async_computation.5 | async-start | bytes 2097152 | tf_op jit(solution)/shard_map/all_to_all | solution.py:1443
  170.1 1.0 copy-start.4
  171.1 30.2 %all-to-all-start.4 = ((bf16[8,256,512]{2,1,0:T(8,128)(2,1)}), bf16[8,256,512]{2,1,0:T(8,128)(2,1)S(1)}, u32[]{:S(2)}, u32[]{:S(2)}) async-start(bf16[8,256,512]{2,1,0:T(8,128)(2,1)} %get-tuple-element.104), calls=%async_computation.4 | async-start | bytes 4194304 | tf_op jit(solution)/shard_map/all_to_all | solution.py:1478
  201.3 1.4 copy-start.1
  206.5 31.8 %all-to-all-start.6 = ((bf16[8,4,272,128]{3,2,1,0:T(8,128)(2,1)}), bf16[8,4,272,128]{3,2,1,0:T(8,128)(2,1)S(1)}, u32[]{:S(2)}, u32[]{:S(2)}) async-start(bf16[8,4,272,128]{3,2,1,0:T(8,128)(2,1)} %get-tuple-element.130), calls=%async_computation.6 | async-start | bytes 4456448 | tf_op jit(solution)/shard_map/all_to_all | solution.py:1518
  210.4 46.0 %copy-start.20 = (bf16[1,256,512]{2,1,0:T(8,128)(2,1)S(1)}, bf16[1,256,512]{2,1,0:T(8,128)(2,1)}, u32[]{:S(2)}) copy-start(bf16[1,256,512]{2,1,0:T(8,128)(2,1)} %get-tuple-element.121) | copy-start | bytes 786436
  210.4 32.4 %collective-permute-start.4 = (bf16[1,384,512]{2,1,0:T(8,128)(2,1)}, bf16[1,384,512]{2,1,0:T(8,128)(2,1)S(1)}, u32[]{:S(2)}, u32[]{:S(2)}) collective-permute-start(bf16[1,384,512]{2,1,0:T(8,128)(2,1)} %get-tuple-element.125), channel_id=1, source_target_pairs={{0,1},{1,0},{2,3},{3,2},{4,5},{5,4},{6,7},{7,6},{8,9},{9,8},{10,11... | collective-permute-start | bytes 1179656 | tf_op jit(solution)/shard_map/ppermute | solution.py:1448
  212.0 46.5 %collective-permute-start.5 = (bf16[1,384,512]{2,1,0:T(8,128)(2,1)}, bf16[1,384,512]{2,1,0:T(8,128)(2,1)S(1)}, u32[]{:S(2)}, u32[]{:S(2)}) collective-permute-start(bf16[1,384,512]{2,1,0:T(8,128)(2,1)} %get-tuple-element.126), channel_id=1, source_target_pairs={{0,2},{1,3},{2,0},{3,1},{4,6},{5,7},{6,4},{7,5},{8,10},{9,11},{10,... | collective-permute-start | bytes 1179656 | tf_op jit(solution)/shard_map/ppermute | solution.py:1448
  214.7 44.2 %collective-permute-start.6 = (bf16[1,384,512]{2,1,0:T(8,128)(2,1)}, bf16[1,384,512]{2,1,0:T(8,128)(2,1)}, u32[]{:S(2)}, u32[]{:S(2)}) collective-permute-start(bf16[1,384,512]{2,1,0:T(8,128)(2,1)} %get-tuple-element.127), channel_id=1, source_target_pairs={{0,3},{1,2},{2,1},{3,0},{4,7},{5,6},{6,5},{7,4},{8,11},{9,10},{10,... | collective-permute-start | bytes 1179656 | tf_op jit(solution)/shard_map/ppermute | solution.py:1448
  238.7 5.0 %collective-permute-start.7 = (bf16[1,272,128]{2,1,0:T(8,128)(2,1)S(1)}, bf16[1,272,128]{2,1,0:T(8,128)(2,1)S(1)}, u32[]{:S(2)}, u32[]{:S(2)}) collective-permute-start(bf16[1,272,128]{2,1,0:T(8,128)(2,1)S(1)} %get-tuple-element.144), channel_id=1, source_target_pairs={{0,1},{1,0},{2,3},{3,2},{4,5},{5,4},{6,7},{7,6},{8,9},{9,8},{10,11... | collective-permute-start | bytes 208904 | tf_op jit(solution)/shard_map/ppermute | solution.py:1448
  240.4 6.6 %collective-permute-start.9 = (bf16[1,272,128]{2,1,0:T(8,128)(2,1)S(1)}, bf16[1,272,128]{2,1,0:T(8,128)(2,1)S(1)}, u32[]{:S(2)}, u32[]{:S(2)}) collective-permute-start(bf16[1,272,128]{2,1,0:T(8,128)(2,1)S(1)} %get-tuple-element.145), channel_id=1, source_target_pairs={{0,3},{1,2},{2,1},{3,0},{4,7},{5,6},{6,5},{7,4},{8,11},{9,10},{10,... | collective-permute-start | bytes 208904 | tf_op jit(solution)/shard_map/ppermute | solution.py:1448
  242.8 34.8 %copy-start.7 = (bf16[1,384,512]{2,1,0:T(8,128)(2,1)}, bf16[1,384,512]{2,1,0:T(8,128)(2,1)S(1)}, u32[]{:S(2)}) copy-start(bf16[1,384,512]{2,1,0:T(8,128)(2,1)S(1)} %collective-permute-done.4.a1) | copy-start | bytes 1179652
  242.8 13.6 %collective-permute-start.8 = (bf16[1,272,128]{2,1,0:T(8,128)(2,1)S(1)}, bf16[1,272,128]{2,1,0:T(8,128)(2,1)S(1)}, u32[]{:S(2)}, u32[]{:S(2)}) collective-permute-start(bf16[1,272,128]{2,1,0:T(8,128)(2,1)S(1)} %get-tuple-element.146), channel_id=1, source_target_pairs={{0,2},{1,3},{2,0},{3,1},{4,6},{5,7},{6,4},{7,5},{8,10},{9,11},{10,... | collective-permute-start | bytes 208904 | tf_op jit(solution)/shard_map/ppermute | solution.py:1448
  243.8 17.8 %collective-permute-start.1 = (bf16[1,256,512]{2,1,0:T(8,128)(2,1)}, bf16[1,256,512]{2,1,0:T(8,128)(2,1)S(1)}, u32[]{:S(2)}, u32[]{:S(2)}) collective-permute-start(bf16[1,256,512]{2,1,0:T(8,128)(2,1)} %get-tuple-element.119), channel_id=1, source_target_pairs={{0,1},{1,0},{2,3},{3,2},{4,5},{5,4},{6,7},{7,6},{8,9},{9,8},{10,11... | collective-permute-start | bytes 786440 | tf_op jit(solution)/shard_map/ppermute | solution.py:1448
  247.0 27.4 %collective-permute-start.2 = (bf16[1,256,512]{2,1,0:T(8,128)(2,1)}, bf16[1,256,512]{2,1,0:T(8,128)(2,1)S(1)}, u32[]{:S(2)}, u32[]{:S(2)}) collective-permute-start(bf16[1,256,512]{2,1,0:T(8,128)(2,1)} %get-tuple-element.120), channel_id=1, source_target_pairs={{0,2},{1,3},{2,0},{3,1},{4,6},{5,7},{6,4},{7,5},{8,10},{9,11},{10,... | collective-permute-start | bytes 786440 | tf_op jit(solution)/shard_map/ppermute | solution.py:1448
  256.4 19.3 %collective-permute-start.3 = (bf16[1,256,512]{2,1,0:T(8,128)(2,1)S(1)}, bf16[1,256,512]{2,1,0:T(8,128)(2,1)S(1)}, u32[]{:S(2)}, u32[]{:S(2)}) collective-permute-start(bf16[1,256,512]{2,1,0:T(8,128)(2,1)S(1)} %copy-done.20), channel_id=1, source_target_pairs={{0,3},{1,2},{2,1},{3,0},{4,7},{5,6},{6,5},{7,4},{8,11},{9,10},{10,... | collective-permute-start | bytes 786440 | tf_op jit(solution)/shard_map/ppermute | solution.py:1448
  258.5 25.0 %copy-start.9 = (bf16[1,272,128]{2,1,0:T(8,128)(2,1)}, bf16[1,272,128]{2,1,0:T(8,128)(2,1)S(1)}, u32[]{:S(2)}) copy-start(bf16[1,272,128]{2,1,0:T(8,128)(2,1)S(1)} %add_convert_fusion.refs_0_) | copy-start | bytes 208900
  258.5 19.1 %copy-start.8 = (bf16[1,384,512]{2,1,0:T(8,128)(2,1)}, bf16[1,384,512]{2,1,0:T(8,128)(2,1)S(1)}, u32[]{:S(2)}) copy-start(bf16[1,384,512]{2,1,0:T(8,128)(2,1)S(1)} %collective-permute-done.5.a2) | copy-start | bytes 1179652
  258.5 17.2 %collective-permute-start.16 = (bf16[1,272,128]{2,1,0:T(8,128)(2,1)S(1)}, bf16[1,272,128]{2,1,0:T(8,128)(2,1)S(1)}, u32[]{:S(2)}, u32[]{:S(2)}) collective-permute-start(bf16[1,272,128]{2,1,0:T(8,128)(2,1)S(1)} %add_convert_fusion.refs_0_), channel_id=1, source_target_pairs={{0,28},{4,24},{8,20},{12,16},{16,12},{20,8},{24,4},{28,0},{1,29},{... | collective-permute-start | bytes 208904 | tf_op jit(solution)/shard_map/ppermute | solution.py:1524
  258.9 18.4 %collective-permute-start.15 = (bf16[1,272,128]{2,1,0:T(8,128)(2,1)S(1)}, bf16[1,272,128]{2,1,0:T(8,128)(2,1)S(1)}, u32[]{:S(2)}, u32[]{:S(2)}) collective-permute-start(bf16[1,272,128]{2,1,0:T(8,128)(2,1)S(1)} %add_convert_fusion.refs_0_), channel_id=1, source_target_pairs={{0,24},{4,28},{8,16},{12,20},{16,8},{20,12},{24,0},{28,4},{1,25},{... | collective-permute-start | bytes 208904 | tf_op jit(solution)/shard_map/ppermute | solution.py:1524
  261.6 19.3 %copy-start.10 = (bf16[1,256,512]{2,1,0:T(8,128)(2,1)}, bf16[1,256,512]{2,1,0:T(8,128)(2,1)S(1)}, u32[]{:S(2)}) copy-start(bf16[1,256,512]{2,1,0:T(8,128)(2,1)S(1)} %collective-permute-done.1.a1) | copy-start | bytes 786436
  261.6 21.8 %collective-permute-start.14 = (bf16[1,272,128]{2,1,0:T(8,128)(2,1)S(1)}, bf16[1,272,128]{2,1,0:T(8,128)(2,1)S(1)}, u32[]{:S(2)}, u32[]{:S(2)}) collective-permute-start(bf16[1,272,128]{2,1,0:T(8,128)(2,1)S(1)} %add_convert_fusion.refs_0_), channel_id=1, source_target_pairs={{0,20},{4,16},{8,28},{12,24},{16,4},{20,0},{24,12},{28,8},{1,21},{... | collective-permute-start | bytes 208904 | tf_op jit(solution)/shard_map/ppermute | solution.py:1524
  274.3 6.5 %copy-start.11 = (bf16[1,256,512]{2,1,0:T(8,128)(2,1)}, bf16[1,256,512]{2,1,0:T(8,128)(2,1)S(1)}, u32[]{:S(2)}) copy-start(bf16[1,256,512]{2,1,0:T(8,128)(2,1)S(1)} %collective-permute-done.2.a2) | copy-start | bytes 786436
  274.3 9.1 %collective-permute-start.13 = (bf16[1,272,128]{2,1,0:T(8,128)(2,1)S(1)}, bf16[1,272,128]{2,1,0:T(8,128)(2,1)S(1)}, u32[]{:S(2)}, u32[]{:S(2)}) collective-permute-start(bf16[1,272,128]{2,1,0:T(8,128)(2,1)S(1)} %add_convert_fusion.refs_0_), channel_id=1, source_target_pairs={{0,16},{4,20},{8,24},{12,28},{16,0},{20,4},{24,8},{28,12},{1,17},{... | collective-permute-start | bytes 208904 | tf_op jit(solution)/shard_map/ppermute | solution.py:1524
  275.7 5.1 %copy-start.12 = (bf16[1,256,512]{2,1,0:T(8,128)(2,1)}, bf16[1,256,512]{2,1,0:T(8,128)(2,1)S(1)}, u32[]{:S(2)}) copy-start(bf16[1,256,512]{2,1,0:T(8,128)(2,1)S(1)} %collective-permute-done.3.a3) | copy-start | bytes 786436
  275.7 7.7 %collective-permute-start.12 = (bf16[1,272,128]{2,1,0:T(8,128)(2,1)S(1)}, bf16[1,272,128]{2,1,0:T(8,128)(2,1)S(1)}, u32[]{:S(2)}, u32[]{:S(2)}) collective-permute-start(bf16[1,272,128]{2,1,0:T(8,128)(2,1)S(1)} %add_convert_fusion.refs_0_), channel_id=1, source_target_pairs={{0,12},{4,8},{8,4},{12,0},{16,28},{20,24},{24,20},{28,16},{1,13},{... | collective-permute-start | bytes 208904 | tf_op jit(solution)/shard_map/ppermute | solution.py:1524
  275.8 7.7 %copy-start.13 = (bf16[1,272,128]{2,1,0:T(8,128)(2,1)}, bf16[1,272,128]{2,1,0:T(8,128)(2,1)S(1)}, u32[]{:S(2)}) copy-start(bf16[1,272,128]{2,1,0:T(8,128)(2,1)S(1)} %collective-permute-done.16.refs_7_) | copy-start | bytes 208900
  275.8 7.7 %collective-permute-start.11 = (bf16[1,272,128]{2,1,0:T(8,128)(2,1)S(1)}, bf16[1,272,128]{2,1,0:T(8,128)(2,1)S(1)}, u32[]{:S(2)}, u32[]{:S(2)}) collective-permute-start(bf16[1,272,128]{2,1,0:T(8,128)(2,1)S(1)} %add_convert_fusion.refs_0_), channel_id=1, source_target_pairs={{0,8},{4,12},{8,0},{12,4},{16,24},{20,28},{24,16},{28,20},{1,9},{5... | collective-permute-start | bytes 208904 | tf_op jit(solution)/shard_map/ppermute | solution.py:1524
  277.3 6.2 %copy-start.14 = (bf16[1,272,128]{2,1,0:T(8,128)(2,1)}, bf16[1,272,128]{2,1,0:T(8,128)(2,1)S(1)}, u32[]{:S(2)}) copy-start(bf16[1,272,128]{2,1,0:T(8,128)(2,1)S(1)} %collective-permute-done.15.refs_6_) | copy-start | bytes 208900
  277.3 6.1 %collective-permute-start.10 = (bf16[1,272,128]{2,1,0:T(8,128)(2,1)S(1)}, bf16[1,272,128]{2,1,0:T(8,128)(2,1)S(1)}, u32[]{:S(2)}, u32[]{:S(2)}) collective-permute-start(bf16[1,272,128]{2,1,0:T(8,128)(2,1)S(1)} %add_convert_fusion.refs_0_), channel_id=1, source_target_pairs={{0,4},{4,0},{8,12},{12,8},{16,20},{20,16},{24,28},{28,24},{1,5},{5... | collective-permute-start | bytes 208904 | tf_op jit(solution)/shard_map/ppermute | solution.py:1524
  283.4 0.6 copy-start.15
  283.4 0.7 copy-start.16
  283.4 0.7 copy-start.17
  283.4 0.7 copy-start.18
  284.1 0.6 copy-start.19
Sparse Core Ops, SparseCore 0:
  10.2 31.7 all-gather.2
  131.0 79.1 reduce-scatter.1
